TPU v7x, 256 devices: a whole 4x4x8 slice. The times are simulated.
256 devices in a mesh: dp: 32 (over x, z), seq: 8 (over y, core).
Axes of the slice: x: 4, y: 4, z: 8, core: 2. Of those that a mesh axis runs over, the one named last changes fastest.
Arguments:
- queries: bfloat16 [65536, 4096], P(('dp', 'seq')), may hold values from -8 to 8
- keys: bfloat16 [65536, 1024], P(('dp', 'seq')), may hold values from -8 to 8
- values: bfloat16 [65536, 1024], P(('dp', 'seq')), may hold values from -6 to 6
- row_offsets: int32 [256, 32], replicated, may hold values from 0 to 256, as said below
- doc_lengths: int32 [32, 32], replicated, may hold values from 0 to 2048, as said below
Outputs:
- attended: bfloat16 [65536, 4096], P(('dp', 'seq'))
Inputs may be any that keep to these rules, and one draw needn't show every extreme that they name: row_offsets[d * 8 + s, g] is the first local row of loader device (d, s) that belongs to group g; a device's rows are ordered by group, so group g's rows run up to the next group's start, or to 256 for the last group. At most 16 rows of one device belong to one group, and the devices (d, s) of one s hold at most 384 rows of one group together; both bounds are reached in every draw. `doc_lengths`: row g lists the lengths of group g's documents in stream order, then zeros; they sum to the number of rows that belong to group g. Every document but a group's last has 128 to 2048 tokens, a group's last has 1 to 2048; some document has exactly 2048.
All inputs are finite; a program needn't handle non-finite values.
Results may differ from a plain program's by a relative error of at most 0.0036.
Values may be sent and summed in bfloat16 or wider, within the bound.
A program may use at most 64 MiB of HBM per device.

v0:
```python
import math

import jax
import jax.numpy as jnp
from jax import lax
from jax.sharding import PartitionSpec as P

HEAD_DIMENSION = 128


NEG_FILL = -1e30
BIG_DOC = 1 << 30


def doc_index(stream, lengths):
    doc_ends = jnp.cumsum(lengths)
    found_ends = jnp.sum((doc_ends[None, :] <= stream[:, None]).astype(jnp.int32), axis=1)
    return jnp.where(stream >= 0, found_ends, -1)


def attend(group_queries, group_keys, group_values, stream, doc_ids, head_size):
    row_count = group_queries.shape[0]
    block_rows = math.gcd(row_count, 512)
    block_count = row_count // block_rows
    kv_local = group_keys.shape[1] // head_size
    queries_per_key_head = group_queries.shape[1] // group_keys.shape[1]
    q_blocks = group_queries.reshape(
        block_count, block_rows, kv_local, queries_per_key_head, head_size
    )
    k_blocks = group_keys.reshape(block_count, block_rows, kv_local, head_size)
    v_blocks = group_values.reshape(block_count, block_rows, kv_local, head_size)
    pos_blocks = stream.reshape(block_count, block_rows)
    doc_blocks = doc_ids.reshape(block_count, block_rows)
    present = pos_blocks >= 0
    first_doc = jnp.min(jnp.where(present, doc_blocks, BIG_DOC), axis=1)
    last_doc = jnp.max(jnp.where(present, doc_blocks, -1), axis=1)
    score_scale = head_size ** (-0.5)

    def one_block(q_index):
        q_here = q_blocks[q_index]
        q_pos = pos_blocks[q_index]
        q_doc = doc_blocks[q_index]

        def score_tile(k_index):
            k_pos = pos_blocks[k_index]
            scores = (
                jnp.einsum(
                    "qhgd,khd->hgqk", q_here, k_blocks[k_index], preferred_element_type=jnp.float32
                )
                * score_scale
            )
            allowed = (
                (q_doc[:, None] == doc_blocks[k_index][None, :])
                & (k_pos[None, :] <= q_pos[:, None])
                & (k_pos[None, :] >= 0)
            )
            return (scores, allowed)

        def touches(k_index):
            return last_doc[k_index] >= first_doc[q_index]

        def raise_top(k_index, row_top):

            def raise_update(row_top):
                scores, allowed = score_tile(k_index)
                return jnp.maximum(row_top, jnp.max(jnp.where(allowed, scores, NEG_FILL), axis=3))

            return lax.cond(touches(k_index), raise_update, lambda kept: kept, row_top)

        row_top = lax.fori_loop(
            0,
            q_index + 1,
            raise_top,
            jnp.full((kv_local, queries_per_key_head, block_rows), NEG_FILL, jnp.float32),
        )

        def accumulate(k_index, carry):

            def accumulate_update(carry):
                weighted, denom = carry
                scores, allowed = score_tile(k_index)
                expo_terms = jnp.where(allowed, jnp.exp(scores - row_top[..., None]), 0.0)
                weighted = weighted + jnp.einsum(
                    "hgqk,khd->qhgd",
                    expo_terms.astype(jnp.bfloat16),
                    v_blocks[k_index],
                    preferred_element_type=jnp.float32,
                )
                return (weighted, denom + jnp.sum(expo_terms, axis=3))

            return lax.cond(touches(k_index), accumulate_update, lambda kept: kept, carry)

        start_carry = (
            jnp.zeros((block_rows, kv_local, queries_per_key_head, head_size), jnp.float32),
            jnp.zeros((kv_local, queries_per_key_head, block_rows), jnp.float32),
        )
        weighted, denom = lax.fori_loop(0, q_index + 1, accumulate, start_carry)
        denom = jnp.where(denom > 0.0, denom, 1.0)
        result = weighted / jnp.transpose(denom, (2, 0, 1))[..., None]
        return result.astype(jnp.bfloat16).reshape(
            block_rows, kv_local * queries_per_key_head * head_size
        )

    return lax.map(one_block, jnp.arange(block_count)).reshape(
        row_count, kv_local * queries_per_key_head * head_size
    )


def on_device(queries, keys, values, row_offsets, doc_lengths):
    dp_count = lax.axis_size("dp")
    seq_count = lax.axis_size("seq")
    tok_dev = queries.shape[0]
    slot_count = 2 * tok_dev // dp_count
    width_q = queries.shape[1]
    my_dp = lax.axis_index("dp")
    my_seq = lax.axis_index("seq")
    ends_all = jnp.concatenate(
        [row_offsets[:, 1:], jnp.full((row_offsets.shape[0], 1), tok_dev, jnp.int32)], axis=1
    )
    counts = ends_all - row_offsets
    my_flat = my_dp * seq_count + my_seq
    my_starts = lax.dynamic_index_in_dim(row_offsets, my_flat, 0, keepdims=False)
    my_counts = lax.dynamic_index_in_dim(counts, my_flat, 0, keepdims=False)
    slot_lane = jnp.arange(slot_count, dtype=jnp.int32)
    usable = slot_lane[None, :] < my_counts[:, None]
    pick_rows = jnp.where(usable, my_starts[:, None] + slot_lane[None, :], 0).reshape(-1)

    def outgoing(rows_in):
        taken_rows = jnp.take(rows_in, pick_rows, axis=0).reshape(
            dp_count, slot_count, rows_in.shape[1]
        )
        return jnp.where(usable[:, :, None], taken_rows, jnp.zeros((), rows_in.dtype))

    column = lax.dynamic_index_in_dim(counts, my_dp, 1, keepdims=False)
    count_grid = jnp.transpose(column.reshape(dp_count, seq_count))
    seq_total = jnp.sum(count_grid, axis=1)
    seq_base = jnp.cumsum(seq_total) - seq_total
    dp_base = jnp.cumsum(count_grid, axis=1) - count_grid
    lengths = lax.dynamic_index_in_dim(doc_lengths, my_dp, 0, keepdims=False)
    slot_stream = jnp.where(
        slot_lane[None, None, :] < count_grid[:, :, None],
        seq_base[:, None, None] + dp_base[:, :, None] + slot_lane[None, None, :],
        -1,
    ).reshape(-1)
    got_q, got_k, got_v = (
        lax.all_to_all(outgoing(queries), "dp", split_axis=0, concat_axis=0, tiled=True),
        lax.all_to_all(outgoing(keys), "dp", split_axis=0, concat_axis=0, tiled=True),
        lax.all_to_all(outgoing(values), "dp", split_axis=0, concat_axis=0, tiled=True),
    )
    got_q = got_q.reshape(dp_count * slot_count, got_q.shape[2])
    got_k = got_k.reshape(dp_count * slot_count, got_k.shape[2])
    got_v = got_v.reshape(dp_count * slot_count, got_v.shape[2])
    group_queries, group_keys, group_values = (
        lax.all_to_all(got_q, "seq", split_axis=1, concat_axis=0, tiled=True),
        lax.all_to_all(got_k, "seq", split_axis=1, concat_axis=0, tiled=True),
        lax.all_to_all(got_v, "seq", split_axis=1, concat_axis=0, tiled=True),
    )
    local_out = attend(
        group_queries,
        group_keys,
        group_values,
        slot_stream,
        doc_index(slot_stream, lengths),
        HEAD_DIMENSION,
    )
    returned = lax.all_to_all(local_out, "seq", split_axis=0, concat_axis=1, tiled=True)
    at_home = lax.all_to_all(
        returned.reshape(dp_count, slot_count, width_q),
        "dp",
        split_axis=0,
        concat_axis=0,
        tiled=True,
    ).reshape(dp_count * slot_count, width_q)
    loader_row = jnp.arange(tok_dev, dtype=jnp.int32)
    owner_group = jnp.sum(
        ((my_starts + my_counts)[None, :] <= loader_row[:, None]).astype(jnp.int32), axis=1
    )
    owner_group = jnp.minimum(owner_group, dp_count - 1)
    source_slot = owner_group * slot_count + loader_row - jnp.take(my_starts, owner_group)
    return jnp.take(at_home, source_slot, axis=0)


def solution(mesh):
    return jax.shard_map(
        on_device,
        mesh=mesh,
        in_specs=(P(("dp", "seq"), None), P(("dp", "seq"), None), P(("dp", "seq"), None), P(), P()),
        out_specs=P(("dp", "seq"), None),
        check_vma=False,
    )
```

profile of v0, /device:TPU:1, one launch (start us, length us, event | category | flops | bytes accessed | tf_op | source)
XLA Modules:
  0.0 824.9 jit_solution(9634387693165675614)
XLA Ops:
  3.1 4.7 gather_fusion.2
  7.8 2.8 gather_fusion.3
  13.6 36.4 %all_to_all.81 = bf16[32,16,1024]{2,1,0:T(8,128)(2,1)} all-to-all(bf16[32,16,1024]{2,1,0:T(8,128)(2,1)S(1)} %get-tuple-element.634), channel_id=1, replica_groups=mesh['dp'=32,'seq'=8] {'dp'}, dimensions={0} | all-to-all | bytes 2097152 | tf_op jit(solution)/shard_map/all_to_all | solution.py:148
  49.9 8.6 %all-to-all-start.2 = ((bf16[32,16,1024]{2,1,0:T(8,128)(2,1)}), bf16[32,16,1024]{2,1,0:T(8,128)(2,1)S(1)}, u32[]{:S(2)}, u32[]{:S(2)}) async-start(bf16[32,16,1024]{2,1,0:T(8,128)(2,1)} %get-tuple-element.635), calls=%async_computation.2 | async-start | bytes 2097152 | tf_op jit(solution)/shard_map/all_to_all | solution.py:147
  58.7 4.4 gather_fusion
  63.1 3.9 select_select_fusion
  67.0 16.3 %all-to-all-done.2 = bf16[32,16,1024]{2,1,0:T(8,128)(2,1)S(1)} async-done(((bf16[32,16,1024]{2,1,0:T(8,128)(2,1)}), bf16[32,16,1024]{2,1,0:T(8,128)(2,1)S(1)}, u32[]{:S(2)}, u32[]{:S(2)}) %all-to-all-start.2) | async-done | bytes 1048608 | tf_op jit(solution)/shard_map/all_to_all | solution.py:147
  83.3 8.6 %all-to-all-start = ((bf16[32,16,4096]{2,1,0:T(8,128)(2,1)}), bf16[32,16,4096]{2,1,0:T(8,128)(2,1)}, u32[]{:S(2)}, u32[]{:S(2)}) async-start(bf16[32,16,4096]{2,1,0:T(8,128)(2,1)} %select_select_fusion), calls=%async_computation | async-start | bytes 8388608 | tf_op jit(solution)/shard_map/all_to_all | solution.py:146
  93.3 91.3 %all-to-all-done = bf16[32,16,4096]{2,1,0:T(8,128)(2,1)} async-done(((bf16[32,16,4096]{2,1,0:T(8,128)(2,1)}), bf16[32,16,4096]{2,1,0:T(8,128)(2,1)}, u32[]{:S(2)}, u32[]{:S(2)}) %all-to-all-start) | async-done | bytes 4194336 | tf_op jit(solution)/shard_map/all_to_all | solution.py:146
  184.6 9.7 %all-to-all-start.5 = ((bf16[512,8,128]{2,0,1:T(8,128)(2,1)}), bf16[512,8,128]{2,0,1:T(8,128)(2,1)S(1)}, u32[]{:S(2)}, u32[]{:S(2)}) async-start(bf16[512,8,128]{2,0,1:T(8,128)(2,1)} %copy.43), calls=%async_computation.5 | async-start | bytes 2097152 | tf_op jit(solution)/shard_map/all_to_all | solution.py:156
  194.3 4.4 copy.50
  198.7 3.4 copy.38
  202.1 7.3 all-to-all-done.5
  209.4 5.3 all-to-all-start.1
  216.3 4.5 compare_select_fusion.7
  220.9 15.9 %compare_and_fusion.2 = (pred[256]{0:T(512)(128)(4,1)}, s32[256]{0:T(256)S(1)}) fusion(s32[256]{0:T(256)S(1)} %convert_reduce_fusion.1, pred[256]{0:T(512)(128)(4,1)S(1)} %get-tuple-element.515, pred[256]{0:T(512)(128)(4,1)S(1)} %get-tuple-element.513, pred[256]{0:T(512)(128)(4,1)S(1)} %get-tuple-element.514, pred[256]{0:T(512)(128)(4,1)S(1)} %get-tuple-element.512, ...), kind=kLoop, calls=%fused_computation.116 | loop fusion | flops 10752 | bytes 9828 | tf_op jit(solution)/shard_map/jit(_take)/and | solution.py:180
  239.3 24.3 %all-to-all-done.1 = bf16[512,8,512]{2,0,1:T(8,128)(2,1)} async-done(((bf16[512,8,512]{2,0,1:T(8,128)(2,1)}), bf16[512,8,512]{2,0,1:T(8,128)(2,1)}, u32[]{:S(2)}, u32[]{:S(2)}) %all-to-all-start.1) | async-done | bytes 4194336 | tf_op jit(solution)/shard_map/all_to_all | solution.py:154
  263.6 5.0 all-to-all-start.3
  271.7 6.5 copy.39
  278.2 5.7 all-to-all-done.3
  283.9 298.3 %while.41 = (s32[]{:T(128)}, bf16[8,512,512]{1,2,0:T(8,128)(2,1)}, s32[8]{0:T(128)S(1)}, bf16[8,512,1,4,128]{1,4,3,0,2:T(8,128)(2,1)}, s32[8,512]{1,0:T(8,128)S(...) while((s32[]{:T(128)}, bf16[8,512,512]{1,2,0:T(8,128)(2,1)}, ...), condition=%wide.region_19.21_spmd, body=%wide.region_8.20_spmd.sunk | while | flops 819729408 | bytes 19173088 | solution.py:104
  289.0 4.0 while.42
  293.1 5.7 while.43
  295.0 3.9 conditional.5
  305.1 8.0 while.42
  313.2 11.5 %while.43 = (s32[]{:T(128)}, f32[512,1,4,128]{0,3,2,1:T(8,128)S(1)}, f32[1,4,512]{2,1,0:T(4,128)S(1)}, s32[]{:T(128)}, s32[8]{0:T(128)S(1)}, /*index=5*/s32[1]{0...) while((s32[]{:T(128)}, ...), condition=%wide.region_18.19_spmd, body=%wide.region_14.18_spmd.sunk | while | flops 546570752 | bytes 12125579 | solution.py:97
  315.0 3.9 conditional.5
  320.7 3.9 conditional.5
  321.1 2.3 fusion.7
  330.9 9.8 %while.42 = (s32[]{:T(128)}, f32[1,4,512]{2,1,0:T(4,128)S(1)}, s32[]{:T(128)}, s32[8]{0:T(128)S(1)}, s32[1]{0:T(128)}, /*index=5*/s32[1,512]{1,0:T(1,128)S(1)}, ...) while((s32[]{:T(128)}, f32[1,4,512]{2,1,0:T(4,128)S(1)}, ...), condition=%wide.region_13.14_spmd, body=%wide.region_9.13_spmd.sunk | while | flops 272630272 | bytes 1230135 | solution.py:70
  340.8 13.4 %while.43 = (s32[]{:T(128)}, f32[512,1,4,128]{0,3,2,1:T(8,128)S(1)}, f32[1,4,512]{2,1,0:T(4,128)S(1)}, s32[]{:T(128)}, s32[8]{0:T(128)S(1)}, /*index=5*/s32[1]{0...) while((s32[]{:T(128)}, ...), condition=%wide.region_18.19_spmd, body=%wide.region_14.18_spmd.sunk | while | flops 546570752 | bytes 12125579 | solution.py:97
  344.5 3.9 conditional.5
  350.3 3.9 conditional.5
  360.3 13.8 %while.42 = (s32[]{:T(128)}, f32[1,4,512]{2,1,0:T(4,128)S(1)}, s32[]{:T(128)}, s32[8]{0:T(128)S(1)}, s32[1]{0:T(128)}, /*index=5*/s32[1,512]{1,0:T(1,128)S(1)}, ...) while((s32[]{:T(128)}, f32[1,4,512]{2,1,0:T(4,128)S(1)}, ...), condition=%wide.region_13.14_spmd, body=%wide.region_9.13_spmd.sunk | while | flops 272630272 | bytes 1230135 | solution.py:70
  374.3 19.1 %while.43 = (s32[]{:T(128)}, f32[512,1,4,128]{0,3,2,1:T(8,128)S(1)}, f32[1,4,512]{2,1,0:T(4,128)S(1)}, s32[]{:T(128)}, s32[8]{0:T(128)S(1)}, /*index=5*/s32[1]{0...) while((s32[]{:T(128)}, ...), condition=%wide.region_18.19_spmd, body=%wide.region_14.18_spmd.sunk | while | flops 546570752 | bytes 12125579 | solution.py:97
  378.0 3.9 conditional.5
  383.7 3.9 conditional.5
  389.4 3.9 conditional.5
  399.5 17.8 %while.42 = (s32[]{:T(128)}, f32[1,4,512]{2,1,0:T(4,128)S(1)}, s32[]{:T(128)}, s32[8]{0:T(128)S(1)}, s32[1]{0:T(128)}, /*index=5*/s32[1,512]{1,0:T(1,128)S(1)}, ...) while((s32[]{:T(128)}, f32[1,4,512]{2,1,0:T(4,128)S(1)}, ...), condition=%wide.region_13.14_spmd, body=%wide.region_9.13_spmd.sunk | while | flops 272630272 | bytes 1230135 | solution.py:70
  417.4 24.8 %while.43 = (s32[]{:T(128)}, f32[512,1,4,128]{0,3,2,1:T(8,128)S(1)}, f32[1,4,512]{2,1,0:T(4,128)S(1)}, s32[]{:T(128)}, s32[8]{0:T(128)S(1)}, /*index=5*/s32[1]{0...) while((s32[]{:T(128)}, ...), condition=%wide.region_18.19_spmd, body=%wide.region_14.18_spmd.sunk | while | flops 546570752 | bytes 12125579 | solution.py:97
  421.1 3.9 conditional.5
  426.9 3.9 conditional.5
  432.6 3.9 conditional.5
  438.3 3.9 conditional.5
  448.4 15.4 %while.42 = (s32[]{:T(128)}, f32[1,4,512]{2,1,0:T(4,128)S(1)}, s32[]{:T(128)}, s32[8]{0:T(128)S(1)}, s32[1]{0:T(128)}, /*index=5*/s32[1,512]{1,0:T(1,128)S(1)}, ...) while((s32[]{:T(128)}, f32[1,4,512]{2,1,0:T(4,128)S(1)}, ...), condition=%wide.region_13.14_spmd, body=%wide.region_9.13_spmd.sunk | while | flops 272630272 | bytes 1230135 | solution.py:70
  464.0 18.9 %while.43 = (s32[]{:T(128)}, f32[512,1,4,128]{0,3,2,1:T(8,128)S(1)}, f32[1,4,512]{2,1,0:T(4,128)S(1)}, s32[]{:T(128)}, s32[8]{0:T(128)S(1)}, /*index=5*/s32[1]{0...) while((s32[]{:T(128)}, ...), condition=%wide.region_18.19_spmd, body=%wide.region_14.18_spmd.sunk | while | flops 546570752 | bytes 12125579 | solution.py:97
  473.2 3.9 conditional.5
  479.0 3.9 conditional.5
  489.0 17.2 %while.42 = (s32[]{:T(128)}, f32[1,4,512]{2,1,0:T(4,128)S(1)}, s32[]{:T(128)}, s32[8]{0:T(128)S(1)}, s32[1]{0:T(128)}, /*index=5*/s32[1,512]{1,0:T(1,128)S(1)}, ...) while((s32[]{:T(128)}, f32[1,4,512]{2,1,0:T(4,128)S(1)}, ...), condition=%wide.region_13.14_spmd, body=%wide.region_9.13_spmd.sunk | while | flops 272630272 | bytes 1230135 | solution.py:70
  506.4 20.8 %while.43 = (s32[]{:T(128)}, f32[512,1,4,128]{0,3,2,1:T(8,128)S(1)}, f32[1,4,512]{2,1,0:T(4,128)S(1)}, s32[]{:T(128)}, s32[8]{0:T(128)S(1)}, /*index=5*/s32[1]{0...) while((s32[]{:T(128)}, ...), condition=%wide.region_18.19_spmd, body=%wide.region_14.18_spmd.sunk | while | flops 546570752 | bytes 12125579 | solution.py:97
  517.5 3.9 conditional.5
  523.3 3.9 conditional.5
  533.3 21.2 %while.42 = (s32[]{:T(128)}, f32[1,4,512]{2,1,0:T(4,128)S(1)}, s32[]{:T(128)}, s32[8]{0:T(128)S(1)}, s32[1]{0:T(128)}, /*index=5*/s32[1,512]{1,0:T(1,128)S(1)}, ...) while((s32[]{:T(128)}, f32[1,4,512]{2,1,0:T(4,128)S(1)}, ...), condition=%wide.region_13.14_spmd, body=%wide.region_9.13_spmd.sunk | while | flops 272630272 | bytes 1230135 | solution.py:70
  554.7 26.5 %while.43 = (s32[]{:T(128)}, f32[512,1,4,128]{0,3,2,1:T(8,128)S(1)}, f32[1,4,512]{2,1,0:T(4,128)S(1)}, s32[]{:T(128)}, s32[8]{0:T(128)S(1)}, /*index=5*/s32[1]{0...) while((s32[]{:T(128)}, ...), condition=%wide.region_18.19_spmd, body=%wide.region_14.18_spmd.sunk | while | flops 546570752 | bytes 12125579 | solution.py:97
  565.8 3.9 conditional.5
  571.5 3.9 conditional.5
  577.3 3.9 conditional.5
  582.2 54.6 %all_to_all.82 = bf16[8,512,512]{1,2,0:T(8,128)(2,1)} all-to-all(bf16[8,512,512]{1,2,0:T(8,128)(2,1)} %get-tuple-element.445), channel_id=1, replica_groups=mesh['dp'=32,'seq'=8] {'seq'}, dimensions={0} | all-to-all | bytes 8388608 | tf_op jit(solution)/shard_map/all_to_all | solution.py:166
  636.8 8.1 copy.47
  644.9 7.4 reshape.412
  652.3 68.8 %all-to-all-start.7 = ((bf16[32,16,4096]{2,1,0:T(8,128)(2,1)}), bf16[32,16,4096]{2,1,0:T(8,128)(2,1)}, u32[]{:S(2)}, u32[]{:S(2)}) async-start(bf16[32,16,4096]{2,1,0:T(8,128)(2,1)} %reshape.412), calls=%async_computation.7 | async-start | bytes 8388608 | tf_op jit(solution)/shard_map/all_to_all | solution.py:167
  721.1 92.5 %all-to-all-done.7 = bf16[32,16,4096]{2,1,0:T(8,128)(2,1)} async-done(((bf16[32,16,4096]{2,1,0:T(8,128)(2,1)}), bf16[32,16,4096]{2,1,0:T(8,128)(2,1)}, u32[]{:S(2)}, u32[]{:S(2)}) %all-to-all-start.7) | async-done | bytes 4194336 | tf_op jit(solution)/shard_map/all_to_all | solution.py:167
  813.6 8.1 gather_fusion.1
  821.7 3.2 broadcast_select_fusion
  (489 shorter events, 240.0 us)
Async XLA Ops:
  0.0 58.7 %copy-start = (bf16[256,4096]{1,0:T(8,128)(2,1)S(1)}, bf16[256,4096]{1,0:T(8,128)(2,1)}, u32[]{:S(2)}) copy-start(bf16[256,4096]{1,0:T(8,128)(2,1)} %param.17) | copy-start | bytes 6291460
  3.1 4.7 copy-start.2
  49.9 33.4 %all-to-all-start.2 = ((bf16[32,16,1024]{2,1,0:T(8,128)(2,1)}), bf16[32,16,1024]{2,1,0:T(8,128)(2,1)S(1)}, u32[]{:S(2)}, u32[]{:S(2)}) async-start(bf16[32,16,1024]{2,1,0:T(8,128)(2,1)} %get-tuple-element.635), calls=%async_computation.2 | async-start | bytes 2097152 | tf_op jit(solution)/shard_map/all_to_all | solution.py:147
  67.0 24.9 %copy-start.3 = (bf16[32,16,1024]{2,1,0:T(8,128)(2,1)S(1)}, bf16[32,16,1024]{2,1,0:T(8,128)(2,1)}, u32[]{:S(2)}) copy-start(bf16[32,16,1024]{2,1,0:T(8,128)(2,1)} %all_to_all.81) | copy-start | bytes 3145732
  83.3 101.3 %all-to-all-start = ((bf16[32,16,4096]{2,1,0:T(8,128)(2,1)}), bf16[32,16,4096]{2,1,0:T(8,128)(2,1)}, u32[]{:S(2)}, u32[]{:S(2)}) async-start(bf16[32,16,4096]{2,1,0:T(8,128)(2,1)} %select_select_fusion), calls=%async_computation | async-start | bytes 8388608 | tf_op jit(solution)/shard_map/all_to_all | solution.py:146
  184.6 24.8 %all-to-all-start.5 = ((bf16[512,8,128]{2,0,1:T(8,128)(2,1)}), bf16[512,8,128]{2,0,1:T(8,128)(2,1)S(1)}, u32[]{:S(2)}, u32[]{:S(2)}) async-start(bf16[512,8,128]{2,0,1:T(8,128)(2,1)} %copy.43), calls=%async_computation.5 | async-start | bytes 2097152 | tf_op jit(solution)/shard_map/all_to_all | solution.py:156
  202.1 12.6 %copy-start.4 = (s32[256,32]{0,1:T(8,128)S(1)}, s32[256,32]{0,1:T(8,128)}, u32[]{:S(2)}) copy-start(s32[256,32]{0,1:T(8,128)} %param.20) | copy-start | bytes 98308
  209.4 54.2 %all-to-all-start.1 = ((bf16[512,8,512]{2,0,1:T(8,128)(2,1)}), bf16[512,8,512]{2,0,1:T(8,128)(2,1)}, u32[]{:S(2)}, u32[]{:S(2)}) async-start(bf16[512,8,512]{2,0,1:T(8,128)(2,1)} %copy.38), calls=%async_computation.1 | async-start | bytes 8388608 | tf_op jit(solution)/shard_map/all_to_all | solution.py:154
  263.6 20.2 %all-to-all-start.3 = ((bf16[512,8,128]{2,0,1:T(8,128)(2,1)}), bf16[512,8,128]{2,0,1:T(8,128)(2,1)}, u32[]{:S(2)}, u32[]{:S(2)}) async-start(bf16[512,8,128]{2,0,1:T(8,128)(2,1)} %copy.42), calls=%async_computation.3 | async-start | bytes 2097152 | tf_op jit(solution)/shard_map/all_to_all | solution.py:155
  652.3 68.8 %copy-start.5 = (s32[256,1]{0,1:T(1,128)S(1)}, s32[256,1]{0,1:T(1,128)}, u32[]{:S(2)}) copy-start(s32[256,1]{0,1:T(1,128)} %get-tuple-element.640) | copy-start | bytes 3076
  652.3 161.3 %all-to-all-start.7 = ((bf16[32,16,4096]{2,1,0:T(8,128)(2,1)}), bf16[32,16,4096]{2,1,0:T(8,128)(2,1)}, u32[]{:S(2)}, u32[]{:S(2)}) async-start(bf16[32,16,4096]{2,1,0:T(8,128)(2,1)} %reshape.412), calls=%async_computation.7 | async-start | bytes 8388608 | tf_op jit(solution)/shard_map/all_to_all | solution.py:167
  813.6 8.1 copy-start.6
  813.6 11.2 %copy-start.1 = (bf16[256,4096]{1,0:T(8,128)(2,1)S(1)}, bf16[256,4096]{1,0:T(8,128)(2,1)}, u32[]{:S(2)}) copy-start(bf16[256,4096]{1,0:T(8,128)(2,1)} %param.17) | copy-start | bytes 6291460
where the time goes:
time: 832 us; the launch traced here: 825 us
  waiting for transfers between devices  237 us (28%)
  local copies, waits for them, and re-layouts  130 us (16%)
  loops' own time  112 us (13%)
  starting transfers between devices  106 us (13%)
  matrix products  99.2 us (12%)
  blocking collectives  91 us (11%)
  other arithmetic  48.9 us (6%)
    all_to_all x1, waiting for transfers between devices, on_device(): lax.all_to_all(returned.reshape(dp_count, slot_count, width_q), 'dp', spl...  92.5 us
    all_to_all x1, waiting for transfers between devices, on_device(): lax.all_to_all(outgoing(queries), 'dp', split_axis=0, concat_axis=0, tile...  91.3 us
    dot_general x38, matrix products, score_tile(): jnp.einsum('qhgd,khd->hgqk', q_here, k_blocks[k_index], preferred_element...  75.8 us
    all_to_all x1, starting transfers between devices, on_device(): lax.all_to_all(returned.reshape(dp_count, slot_count, width_q), 'dp', spl...  68.8 us
    all_to_all x1, blocking collectives, on_device(): lax.all_to_all(local_out, 'seq', split_axis=0, concat_axis=1, tiled=True)  54.6 us
    dynamic_slice x80, local copies, waits for them, and re-layouts, touches(): return last_doc[k_index] >= first_doc[q_index]  48.8 us
    another operation x8, loops' own time, one_block(): weighted, denom = lax.fori_loop(0, q_index + 1, accumulate, start_carry)  44.4 us
    another operation x8, loops' own time, one_block(): lax.fori_loop(0, q_index + 1, raise_top, jnp.full((kv_local, queries_per_...  44.4 us
  transfers between devices with their start and end apart: 6, of which 6 were waited for; matrix products, arithmetic and copies ran while one was open for 6% of the time, Pallas kernels for 0%

commit v1 on v0

v1 whole, which is shorter than its diff:
```python
import functools
import math

import jax
import jax.numpy as jnp
from jax import lax
from jax.experimental import pallas as pl
from jax.experimental.pallas import tpu as pltpu
from jax.sharding import PartitionSpec as P

MESH = pl.DeviceIdType.MESH
HEAD = 128
NEG_FILL = -1e30
BIG = 1 << 30
VMEM_LIMIT = 50 * 1024 * 1024


class Sizes:
    def __init__(self, dp_count, seq_count, tok, width_q, width_k):
        self.groups = dp_count
        self.S = seq_count
        self.Z = width_k // HEAD
        self.X = dp_count // self.Z
        self.tok = tok
        self.slots = 2 * tok // dp_count
        self.seg = 3 * tok // 2
        self.G = width_q // width_k
        self.qw = self.G * HEAD
        self.W = self.qw + 2 * HEAD
        self.flat = self.groups * self.slots
        self.per_s = self.X * self.Z * self.slots
        self.rows = self.S * self.seg
        self.blk = math.gcd(self.rows, 256)
        self.nb = self.rows // self.blk


def near_first(count):
    order = [0]
    for dist in range(1, count // 2 + 1):
        order.append(dist)
        if count - dist != dist:
            order.append(count - dist)
    return order


def greet(n, x, z, s):
    barrier = pltpu.get_barrier_semaphore()
    plane = x * n.S + s
    count = n.X * n.S

    def one_plane(t, carry):
        p = lax.rem(plane + t, count)
        pl.semaphore_signal(
            barrier, inc=1, device_id=((p // n.S) * n.Z + z, lax.rem(p, n.S)), device_id_type=MESH
        )
        return carry

    lax.fori_loop(1, count, one_plane, 0)

    def one_line(t, carry):
        zt = lax.rem(z + t, n.Z)
        pl.semaphore_signal(barrier, inc=1, device_id=(x * n.Z + zt, s), device_id_type=MESH)
        return carry

    lax.fori_loop(1, n.Z, one_line, 0)
    pl.semaphore_wait(barrier, count - 1 + n.Z - 1)


def in_kernel(n, q_ref, k_ref, v_ref, idx_ref, out_ref, zbuf, sbuf, zsend, zrecv, psend, precv, own_sem):
    dp, s = lax.axis_index("dp"), lax.axis_index("seq")
    x, z = dp // n.Z, lax.rem(dp, n.Z)
    plane = x * n.S + s
    count = n.X * n.S
    mine = s * n.X + x
    qw = n.qw
    order = near_first(n.Z)

    def parts(zt, delta):
        return (
            (q_ref.at[:, pl.ds(pl.multiple_of(zt * qw, qw), qw)], zbuf.at[delta, :, pl.ds(0, qw)]),
            (k_ref.at[:, pl.ds(pl.multiple_of(zt * HEAD, HEAD), HEAD)], zbuf.at[delta, :, pl.ds(qw, HEAD)]),
            (v_ref.at[:, pl.ds(pl.multiple_of(zt * HEAD, HEAD), HEAD)], zbuf.at[delta, :, pl.ds(qw + HEAD, HEAD)]),
        )

    for src, dst in parts(z, 0):
        pltpu.make_async_copy(src, dst, zrecv.at[0]).start()
    greet(n, x, z, s)
    for delta in order[1:]:
        zt = lax.rem(z + delta, n.Z)
        for src, dst in parts(zt, delta):
            pltpu.make_async_remote_copy(
                src_ref=src,
                dst_ref=dst,
                send_sem=zsend.at[delta],
                recv_sem=zrecv.at[delta],
                device_id=(x * n.Z + zt, s),
                device_id_type=MESH,
            ).start()

    lane = lax.broadcasted_iota(jnp.int32, (n.flat, n.tok), 1)
    for step, delta in enumerate(order):
        pltpu.make_async_copy(zbuf.at[delta], zbuf.at[delta], zrecv.at[delta]).wait()
        pick = (lane == idx_ref[:, step : step + 1]).astype(jnp.bfloat16)
        padded = jnp.dot(pick, zbuf[delta], preferred_element_type=jnp.float32).astype(jnp.bfloat16)
        sbuf[delta] = padded.reshape(n.groups, n.slots, n.W)
        z_src = lax.rem(z - delta + n.Z, n.Z)
        pltpu.make_async_copy(sbuf.at[delta, plane], out_ref.at[mine, z_src], own_sem).start()

        def send(t, carry):
            p = lax.rem(plane + t, count)
            pltpu.make_async_remote_copy(
                src_ref=sbuf.at[delta, p],
                dst_ref=out_ref.at[mine, z_src],
                send_sem=psend.at[t],
                recv_sem=precv.at[mine],
                device_id=((p // n.S) * n.Z + z, lax.rem(p, n.S)),
                device_id_type=MESH,
            ).start()
            return carry

        lax.fori_loop(1, count, send, 0)

    pltpu.make_async_copy(out_ref.at[mine], out_ref.at[mine], own_sem).wait()

    def finish(t, carry):
        p = lax.rem(plane + t, count)
        src = lax.rem(p, n.S) * n.X + p // n.S
        pltpu.make_async_copy(out_ref.at[src], out_ref.at[src], precv.at[src]).wait()
        pltpu.make_async_copy(out_ref.at[src], out_ref.at[src], psend.at[t]).wait()
        return carry

    lax.fori_loop(1, count, finish, 0)
    for delta in order[1:]:
        pltpu.make_async_copy(zbuf.at[delta], zbuf.at[delta], zsend.at[delta]).wait()


def route_in(n, q, k, v, idx_cols):
    anyspace = pl.BlockSpec(memory_space=pl.ANY)
    return pl.pallas_call(
        functools.partial(in_kernel, n),
        out_shape=jax.ShapeDtypeStruct((n.S * n.X, n.Z, n.slots, n.W), jnp.bfloat16),
        in_specs=[anyspace, anyspace, anyspace, pl.BlockSpec(memory_space=pltpu.VMEM)],
        out_specs=anyspace,
        scratch_shapes=[
            pltpu.VMEM((n.Z, n.tok, n.W), jnp.bfloat16),
            pltpu.VMEM((n.Z, n.groups, n.slots, n.W), jnp.bfloat16),
            pltpu.SemaphoreType.DMA((n.Z,)),
            pltpu.SemaphoreType.DMA((n.Z,)),
            pltpu.SemaphoreType.DMA((n.X * n.S,)),
            pltpu.SemaphoreType.DMA((n.X * n.S,)),
            pltpu.SemaphoreType.DMA,
        ],
        compiler_params=pltpu.CompilerParams(
            collective_id=0, has_side_effects=True, vmem_limit_bytes=VMEM_LIMIT
        ),
        name="route_in",
    )(q, k, v, idx_cols)


def attend_kernel(n, base_ref, tot_ref, low_ref, last_ref, rows_ref, dst_ref, ends_ref, out_ref,
                  rbuf, comp, strip, top, total, acc, sems):
    copies = [pltpu.make_async_copy(rows_ref.at[s], rbuf.at[s], sems.at[s]) for s in range(n.S)]
    for c in copies:
        c.start()
    sub = lax.broadcasted_iota(jnp.int32, (n.seg, n.per_s), 0)
    for s in range(n.S):
        copies[s].wait()
        pick = (sub == dst_ref[s : s + 1, :]).astype(jnp.bfloat16)
        comp[s * n.seg : (s + 1) * n.seg, :] = jnp.dot(
            pick, rbuf[s], preferred_element_type=jnp.float32
        ).astype(jnp.bfloat16)

    blk, qw = n.blk, n.qw
    half = min(128, blk)
    gain = HEAD ** -0.5 * math.log2(math.e)

    def positions(b, shape, dim, missing):
        u = lax.broadcasted_iota(jnp.int32, shape, dim) + b * blk
        s1 = (b * blk) // n.seg
        s2 = jnp.minimum(s1 + 1, n.S - 1)
        r1 = u - s1 * n.seg
        r2 = r1 - n.seg
        first = jnp.where(r1 < tot_ref[s1], base_ref[s1] + r1, missing)
        second = jnp.where(r2 < tot_ref[s2], base_ref[s2] + r2, missing)
        return jnp.where(r1 < n.seg, first, second)

    def q_block(i, carry):
        start = pl.multiple_of(i * blk, blk)

        @pl.when(last_ref[i] < 0)
        def _():
            out_ref[pl.ds(start, blk), :] = jnp.zeros((blk, qw), out_ref.dtype)

        @pl.when(last_ref[i] >= 0)
        def _():
            q_pos = positions(i, (blk, 1), 0, -1)
            ends = ends_ref[...]
            q_low = jnp.max(jnp.where(ends <= q_pos, ends, 0), axis=1, keepdims=True)
            top[...] = jnp.full(top.shape, NEG_FILL, jnp.float32)
            total[...] = jnp.zeros(total.shape, jnp.float32)
            acc[...] = jnp.zeros(acc.shape, jnp.float32)
            low = low_ref[i]

            def scores(b, carry):
                @pl.when(last_ref[b] >= low)
                def _():
                    k_pos = positions(b, (1, blk), 1, BIG)
                    allowed = (k_pos >= q_low) & (k_pos <= q_pos)
                    k_start = pl.multiple_of(b * blk, blk)
                    keys = comp[pl.ds(k_start, blk), qw : qw + HEAD]
                    for h in range(n.G):
                        sc = lax.dot_general(
                            comp[pl.ds(start, blk), h * HEAD : (h + 1) * HEAD],
                            keys,
                            (((1,), (1,)), ((), ())),
                            preferred_element_type=jnp.float32,
                        )
                        sc = jnp.where(allowed, sc, NEG_FILL)
                        strip[b, h] = sc
                        best = top[h]
                        for c in range(0, blk, half):
                            best = jnp.maximum(best, sc[:, c : c + half])
                        top[h] = best

                return carry

            lax.fori_loop(0, i + 1, scores, 0)
            for h in range(n.G):
                row = jnp.max(top[h], axis=1, keepdims=True) * gain
                top[h] = jnp.broadcast_to(row, (blk, half))

            def weigh(b, carry):
                @pl.when(last_ref[b] >= low)
                def _():
                    k_start = pl.multiple_of(b * blk, blk)
                    vals = comp[pl.ds(k_start, blk), qw + HEAD : qw + 2 * HEAD]
                    for h in range(n.G):
                        w = jnp.exp2(strip[b, h] * gain - top[h][:, 0:1])
                        sums = total[h]
                        for c in range(0, blk, half):
                            sums = sums + w[:, c : c + half]
                        total[h] = sums
                        acc[h] += jnp.dot(w.astype(jnp.bfloat16), vals, preferred_element_type=jnp.float32)

                return carry

            lax.fori_loop(0, i + 1, weigh, 0)
            for h in range(n.G):
                denom = jnp.sum(total[h], axis=1, keepdims=True)
                denom = jnp.where(denom > 0.0, denom, 1.0)
                out_ref[pl.ds(start, blk), h * HEAD : (h + 1) * HEAD] = (acc[h] / denom).astype(out_ref.dtype)

        return carry

    lax.fori_loop(0, n.nb, q_block, 0)


def attend(n, rows, dst, base, tot, low, last, ends):
    smem = pl.BlockSpec(memory_space=pltpu.SMEM)
    vmem = pl.BlockSpec(memory_space=pltpu.VMEM)
    half = min(128, n.blk)
    return pl.pallas_call(
        functools.partial(attend_kernel, n),
        out_shape=jax.ShapeDtypeStruct((n.rows, n.qw), jnp.bfloat16),
        in_specs=[smem, smem, smem, smem, pl.BlockSpec(memory_space=pl.ANY), vmem, vmem],
        out_specs=vmem,
        scratch_shapes=[
            pltpu.VMEM((n.S, n.per_s, n.W), jnp.bfloat16),
            pltpu.VMEM((n.rows, n.W), jnp.bfloat16),
            pltpu.VMEM((n.nb, n.G, n.blk, n.blk), jnp.float32),
            pltpu.VMEM((n.G, n.blk, half), jnp.float32),
            pltpu.VMEM((n.G, n.blk, half), jnp.float32),
            pltpu.VMEM((n.G, n.blk, HEAD), jnp.float32),
            pltpu.SemaphoreType.DMA((n.S,)),
        ],
        compiler_params=pltpu.CompilerParams(vmem_limit_bytes=VMEM_LIMIT),
        name="attend",
    )(base, tot, low, last, rows, dst, ends)


def out_kernel(n, att_ref, dst_ref, idx_ref, out_ref, ubuf, rbuf, fbuf, usend, urecv, fsend, frecv):
    dp, s = lax.axis_index("dp"), lax.axis_index("seq")
    x, z = dp // n.Z, lax.rem(dp, n.Z)
    plane = x * n.S + s
    count = n.X * n.S
    qw = n.qw
    order = near_first(n.Z)[::-1]

    lane = lax.broadcasted_iota(jnp.int32, (n.per_s, n.seg), 1)
    for part in range(n.S):
        pick = (lane == dst_ref[:, part : part + 1]).astype(jnp.bfloat16)
        spread = jnp.dot(
            pick, att_ref[part * n.seg : (part + 1) * n.seg, :], preferred_element_type=jnp.float32
        ).astype(jnp.bfloat16)
        ubuf[part] = spread.reshape(n.X, n.Z, n.slots, qw)
    greet(n, x, z, s)

    for delta in order:
        zt = lax.rem(z + delta, n.Z)
        pltpu.make_async_copy(ubuf.at[s, x, zt], rbuf.at[delta, plane], urecv.at[delta]).start()

        def send(t, carry):
            p = lax.rem(plane + t, count)
            pltpu.make_async_remote_copy(
                src_ref=ubuf.at[lax.rem(p, n.S), p // n.S, zt],
                dst_ref=rbuf.at[delta, plane],
                send_sem=usend.at[delta],
                recv_sem=urecv.at[delta],
                device_id=((p // n.S) * n.Z + z, lax.rem(p, n.S)),
                device_id_type=MESH,
            ).start()
            return carry

        lax.fori_loop(1, count, send, 0)

    sub = lax.broadcasted_iota(jnp.int32, (n.tok, n.flat), 0)
    columns = pl.ds(pl.multiple_of(z * qw, qw), qw)
    for step, delta in enumerate(order):
        zt = lax.rem(z + delta, n.Z)
        pltpu.make_async_copy(rbuf.at[delta], rbuf.at[delta], urecv.at[delta]).wait()
        pick = (sub == idx_ref[step : step + 1, :]).astype(jnp.bfloat16)
        fbuf[delta] = jnp.dot(
            pick, rbuf[delta].reshape(n.flat, qw), preferred_element_type=jnp.float32
        ).astype(jnp.bfloat16)
        if delta == 0:
            pltpu.make_async_copy(fbuf.at[0], out_ref.at[:, columns], frecv.at[0]).start()
        else:
            pltpu.make_async_remote_copy(
                src_ref=fbuf.at[delta],
                dst_ref=out_ref.at[:, columns],
                send_sem=fsend.at[delta],
                recv_sem=frecv.at[delta],
                device_id=(x * n.Z + zt, s),
                device_id_type=MESH,
            ).start()

    for delta in order:
        pltpu.make_async_copy(fbuf.at[delta], fbuf.at[delta], frecv.at[delta]).wait()
        if delta != 0:
            pltpu.make_async_copy(fbuf.at[delta], fbuf.at[delta], fsend.at[delta]).wait()
        some = rbuf.at[delta, pl.ds(0, count - 1)]
        pltpu.make_async_copy(some, some, usend.at[delta]).wait()


def route_out(n, att, dst_cols, idx):
    vmem = pl.BlockSpec(memory_space=pltpu.VMEM)
    return pl.pallas_call(
        functools.partial(out_kernel, n),
        out_shape=jax.ShapeDtypeStruct((n.tok, n.Z * n.qw), jnp.bfloat16),
        in_specs=[vmem, vmem, vmem],
        out_specs=pl.BlockSpec(memory_space=pl.ANY),
        scratch_shapes=[
            pltpu.VMEM((n.S, n.X, n.Z, n.slots, n.qw), jnp.bfloat16),
            pltpu.VMEM((n.Z, n.groups, n.slots, n.qw), jnp.bfloat16),
            pltpu.VMEM((n.Z, n.tok, n.qw), jnp.bfloat16),
            pltpu.SemaphoreType.DMA((n.Z,)),
            pltpu.SemaphoreType.DMA((n.Z,)),
            pltpu.SemaphoreType.DMA((n.Z,)),
            pltpu.SemaphoreType.DMA((n.Z,)),
        ],
        compiler_params=pltpu.CompilerParams(
            collective_id=1, has_side_effects=True, vmem_limit_bytes=VMEM_LIMIT
        ),
        name="route_out",
    )(att, dst_cols, idx)


def on_device(queries, keys, values, row_offsets, doc_lengths):
    n = Sizes(lax.axis_size("dp"), lax.axis_size("seq"), queries.shape[0], queries.shape[1], keys.shape[1])
    dp, s = lax.axis_index("dp"), lax.axis_index("seq")
    x, z = dp // n.Z, lax.rem(dp, n.Z)
    group = x * n.S + s
    row_ends = jnp.concatenate(
        [row_offsets[:, 1:], jnp.full((row_offsets.shape[0], 1), n.tok, jnp.int32)], axis=1
    )
    counts = row_ends - row_offsets
    slot = jnp.arange(n.slots, dtype=jnp.int32)

    def line(table):
        grid = table.reshape(n.X, n.Z, n.S, n.groups)
        return lax.dynamic_slice(grid, (x, 0, s, 0), (1, n.Z, 1, n.groups)).reshape(n.Z, n.groups)

    line_starts, line_counts = line(row_offsets), line(counts)
    idx = jnp.where(
        slot[None, None, :] < line_counts[:, :, None], line_starts[:, :, None] + slot[None, None, :], -1
    ).reshape(n.Z, n.flat)
    near = jnp.asarray(near_first(n.Z), jnp.int32)
    idx_in = jnp.transpose(jnp.take(idx, lax.rem(z - near + n.Z, n.Z), axis=0))
    idx_out = jnp.take(idx, lax.rem(z + near[::-1], n.Z), axis=0)

    column = lax.dynamic_index_in_dim(counts, group, 1, keepdims=False)
    count_grid = jnp.transpose(column.reshape(n.groups, n.S))
    tot = jnp.sum(count_grid, axis=1)
    base = jnp.cumsum(tot) - tot
    dp_base = jnp.cumsum(count_grid, axis=1) - count_grid
    dst = jnp.where(
        slot[None, None, :] < count_grid[:, :, None], dp_base[:, :, None] + slot[None, None, :], -1
    ).reshape(n.S, n.per_s)
    ends = jnp.cumsum(lax.dynamic_index_in_dim(doc_lengths, group, 0, keepdims=False))

    u = jnp.arange(n.rows, dtype=jnp.int32).reshape(n.S, n.seg)
    r = u - u[:, :1]
    pos = jnp.where(r < tot[:, None], base[:, None] + r, -1).reshape(n.nb, n.blk)
    last = jnp.max(pos, axis=1)
    first = jnp.min(jnp.where(pos >= 0, pos, BIG), axis=1)
    low = jnp.max(jnp.where(ends[None, :] <= first[:, None], ends[None, :], 0), axis=1)

    rows = route_in(n, queries, keys, values, idx_in)
    att = attend(
        n, rows.reshape(n.S, n.per_s, n.W), dst, base, tot, low, last, ends.reshape(1, -1)
    )
    return route_out(n, att, jnp.transpose(dst), idx_out)


def solution(mesh):
    return jax.shard_map(
        on_device,
        mesh=mesh,
        in_specs=(P(("dp", "seq"), None), P(("dp", "seq"), None), P(("dp", "seq"), None), P(), P()),
        out_specs=P(("dp", "seq"), None),
        check_vma=False,
    )
```

time: 832 us -> 223 us (0.27)
  waiting for transfers between devices: 237 us -> 0 us
  Pallas kernels: 0 us -> 212 us
  local copies, waits for them, and re-layouts: 130 us -> 7.89 us
  loops' own time: 112 us -> 0 us
  starting transfers between devices: 106 us -> 0 us
  matrix products: 99.2 us -> 0 us
  blocking collectives: 91 us -> 0 us
  other arithmetic: 48.9 us -> 2.02 us
    all_to_all x6 -> x0, waiting for transfers between devices: 237 us -> none  [the longest x1 92.5 us: on_device(): lax.all_to_all(returned.reshape(dp_count, slot_count, width_q), 'dp', spl...]
    pallas_call x0 -> x3, Pallas kernels: none -> 212 us  [the longest x1 95.6 us: route_in(): pl.pallas_call(functools.partial(in_kernel, n), out_shape=jax.ShapeDtypeS...]
    another operation x89 -> x0, loops' own time: 112 us -> none  [the longest x8 44.4 us: one_block(): weighted, denom = lax.fori_loop(0, q_index + 1, accumulate, start_carry)]
    all_to_all x6 -> x0, starting transfers between devices: 106 us -> none  [the longest x1 68.8 us: on_device(): lax.all_to_all(returned.reshape(dp_count, slot_count, width_q), 'dp', spl...]
    dot_general x57 -> x0, matrix products: 99.2 us -> none  [the longest x38 75.8 us: score_tile(): jnp.einsum('qhgd,khd->hgqk', q_here, k_blocks[k_index], preferred_element...]
    all_to_all x2 -> x0, blocking collectives: 91 us -> none  [the longest x1 54.6 us: on_device(): lax.all_to_all(local_out, 'seq', split_axis=0, concat_axis=1, tiled=True)]
    dynamic_slice x150 -> x3, local copies, waits for them, and re-layouts: 65 us -> 0.2 us  [the longest x1 0.18 us: on_device(): column = lax.dynamic_index_in_dim(counts, group, 1, keepdims=False)]
    and x40 -> x1, other arithmetic: 27.7 us -> 0.69 us  [on_device(): idx_out = jnp.take(idx, lax.rem(z + near[::-1], n.Z), axis=0)]
  transfers between devices with their start and end apart: 6 -> 0, of which waited for: 6 -> 0; matrix products, arithmetic and copies ran while one was open for 6% -> 0% of each run, Pallas kernels for 0% -> 0%
where the time goes in v1:
time: 223 us; the launch traced here: 222 us
  Pallas kernels  212 us (95%)
  local copies, waits for them, and re-layouts  7.89 us (4%)
    pallas_call x1, Pallas kernels, route_in(): pl.pallas_call(functools.partial(in_kernel, n), out_shape=jax.ShapeDtypeS...  95.6 us
    pallas_call x1, Pallas kernels, route_out(): pl.pallas_call(functools.partial(out_kernel, n), out_shape=jax.ShapeDtype...  77.1 us
    pallas_call x1, Pallas kernels, attend(): pl.pallas_call(functools.partial(attend_kernel, n), out_shape=jax.ShapeDt...  39.3 us
    unnamed x12, local copies, waits for them, and re-layouts  5.56 us

profile of v1, /device:TPU:1, one launch (start us, length us, event | category | flops | bytes accessed | tf_op | source)
XLA Modules:
  0.0 222.2 jit_solution(87477002198474605)
XLA Ops:
  0.0 0.0 copy-start
  0.0 0.0 copy-start.3
  0.0 0.0 copy-start.2
  0.0 0.7 copy-done
  0.7 0.2 broadcast_in_dim.48.ends_ref
  0.9 0.7 compare_and_fusion
  1.7 0.1 slice_reduce_fusion
  1.8 0.1 lt.88
  1.9 0.9 copy.57
  2.7 0.1 slice.14
  2.9 0.2 dynamic-slice_reduce_fusion
  3.1 0.1 copy.59
  3.1 0.1 copy.61
  3.2 0.1 reshape.85
  3.3 0.2 reduce-window.8
  3.5 0.1 copy.64
  3.6 0.2 reduce_window_sum.25
  3.8 0.1 add_select_fusion
  3.9 0.1 fusion.5
  4.0 0.2 select_reduce_fusion.low_ref
  4.2 0.1 copy.66
  4.3 0.1 fusion
  4.4 0.1 copy.62
  4.5 0.6 gather_fusion.1
  5.1 0.6 gather_fusion
  5.6 0.1 broadcast_select_fusion.1
  5.7 0.1 broadcast_select_fusion.idx_ref
  5.8 0.1 copy.67.dst_ref
  5.9 0.1 copy.63
  6.0 0.0 copy-done.3
  6.0 0.0 copy-done.2
  6.0 0.0 copy-start.4
  6.0 1.0 copy-done.4
  7.1 95.6 %route_in.1 = bf16[32,8,16,768]{3,2,1,0:T(8,128)(2,1)} custom-call(bf16[256,4096]{1,0:T(8,128)(2,1)S(1)} %copy-done.2, bf16[256,1024]{1,0:T(8,128)(2,1)S(1)} %copy-done.3, bf16[256,1024]{1,0:T(8,128)(2,1)S(1)} %copy-done.4, s32[512,8]{1,0:T(8,128)S(1)} %bitcast.31), custom_call_target="tpu_custom_call" | custom-call | tf_op jit(solution)/shard_map/route_in/pallas_call | solution.py:139
  102.7 39.3 %attend.1.att_ref = bf16[3072,512]{1,0:T(8,128)(2,1)S(1)} custom-call(s32[8]{0:T(128)S(1)} %bitcast_subtract_fusion.base_ref, s32[8]{0:T(128)S(1)} %reduce_sum.9.tot_ref, s32[12]{0:T(128)S(1)} %select_reduce_fusion.low_ref, s32[12]{0:T(128)S(1)} %get-tuple-element.6.last_ref, bf16[8,512,768]{2,1,0:T(8,128)(2,1)} %bitcast.34, s32[8,512]{1,0:T(8,128)S(1)} %copy.67.dst_ref, ...), custom_call_target="tpu_custom_call" | custom-call | tf_op jit(solution)/shard_map/attend/pallas_call | solution.py:262
  142.1 0.0 copy-start.1
  142.1 1.7 copy-done.1
  143.7 77.1 %route_out.1 = bf16[256,4096]{1,0:T(8,128)(2,1)S(1)} custom-call(bf16[3072,512]{1,0:T(8,128)(2,1)} %copy-done.1, s32[512,8]{1,0:T(8,128)S(1)} %bitcast.30, s32[8,512]{1,0:T(8,128)S(1)} %broadcast_select_fusion.idx_ref), custom_call_target="tpu_custom_call" | custom-call | tf_op jit(solution)/shard_map/route_out/pallas_call | solution.py:347
  220.9 1.3 copy.71
  (11 shorter events, 0.1 us)
Async XLA Ops:
  0.0 0.7 copy-start
  0.0 6.0 %copy-start.3 = (bf16[256,1024]{1,0:T(8,128)(2,1)S(1)}, bf16[256,1024]{1,0:T(8,128)(2,1)}, u32[]{:S(2)}) copy-start(bf16[256,1024]{1,0:T(8,128)(2,1)} %k_ref.1) | copy-start | bytes 1572868
  0.0 6.0 %copy-start.2 = (bf16[256,4096]{1,0:T(8,128)(2,1)S(1)}, bf16[256,4096]{1,0:T(8,128)(2,1)}, u32[]{:S(2)}) copy-start(bf16[256,4096]{1,0:T(8,128)(2,1)} %q_ref.1) | copy-start | bytes 6291460
  6.0 1.0 copy-start.4
  142.1 1.7 copy-start.1

commit v2 on v0

v2 whole, which is shorter than its diff:
```python
import functools
import math

import jax
import jax.numpy as jnp
from jax import lax
from jax.experimental import pallas as pl
from jax.experimental.pallas import tpu as pltpu
from jax.sharding import PartitionSpec as P

MESH = pl.DeviceIdType.MESH
HEAD = 128
NEG_FILL = -1e30
BIG = 1 << 30
VMEM_LIMIT = 54 * 1024 * 1024


class Sizes:
    def __init__(self, dp_count, seq_count, tok, width_q, width_k, groups):
        self.groups = groups
        self.S = seq_count
        self.Z = width_k // HEAD
        self.X = dp_count // self.Z
        self.tok = tok
        self.slots = 2 * tok // groups
        self.seg = 3 * dp_count * tok // (2 * groups)
        self.G = width_q // width_k
        self.qw = self.G * HEAD
        self.nh = self.G // 2
        self.hw = self.nh * HEAD
        self.widths = (self.hw + 2 * HEAD, self.hw)
        self.flat = self.groups * self.slots
        self.per_s = self.X * self.Z * self.slots
        self.rows = self.S * self.seg
        self.blk = 2 * self.seg // 3
        self.nb = self.rows // self.blk
        self.pad = 3 * self.blk
        self.wide = 4 * self.blk
        order = [0]
        runs = [(0, 1)]
        for dist in range(1, self.Z // 2 + 1):
            at = len(order)
            order.append(dist)
            if self.Z - dist != dist:
                order.append(self.Z - dist)
            runs.append((at, len(order)))
        self.order = order
        self.runs = runs


def greet(n, x, z, s):
    barrier = pltpu.get_barrier_semaphore()
    plane = x * n.S + s
    count = n.X * n.S

    def one_plane(t, carry):
        p = lax.rem(plane + t, count)
        pl.semaphore_signal(
            barrier, inc=1, device_id=((p // n.S) * n.Z + z, lax.rem(p, n.S)), device_id_type=MESH
        )
        return carry

    lax.fori_loop(1, count, one_plane, 0)

    def one_line(t, carry):
        zt = lax.rem(z + t, n.Z)
        pl.semaphore_signal(barrier, inc=1, device_id=(x * n.Z + zt, s), device_id_type=MESH)
        return carry

    lax.fori_loop(1, n.Z, one_line, 0)
    pl.semaphore_wait(barrier, count - 1 + n.Z - 1)


def fused_kernel(n, base_ref, tot_ref, q_ref, k_ref, v_ref, idx_cols, idx_rows, dst_cols, dst_rows, ends_ref, kpos_ref,
                 out_ref, zb0, zb1, sb0, sb1, rc0, rc1, qbuf, kbuf, vbuf, strip, top, acc, qpos, qlow, obuf, ub, rb, fb,
                 zsend, zrecv, psend, precv, usend, urecv, fsend, frecv):
    dp, s = lax.axis_index("dp"), lax.axis_index("seq")
    x, z = dp // n.Z, lax.rem(dp, n.Z)
    plane = x * n.S + s
    count = n.X * n.S
    mine = s * n.X + x
    blk, hw, wide = n.blk, n.hw, n.wide
    half = min(128, blk)
    gain = HEAD ** -0.5 * math.log2(math.e)
    zb, sb, rc = (zb0, zb1), (sb0, sb1), (rc0, rc1)

    def done(ref, sem):
        pltpu.make_async_copy(ref, ref, sem).wait()

    def remote(src, dst, send, recv, dp_to, s_to):
        pltpu.make_async_remote_copy(
            src_ref=src, dst_ref=dst, send_sem=send, recv_sem=recv,
            device_id=(dp_to, s_to), device_id_type=MESH,
        ).start()

    def to_plane(body):
        def one(t, carry):
            p = lax.rem(plane + t, count)
            body(p // n.S, lax.rem(p, n.S))
            return carry

        lax.fori_loop(1, count, one, 0)

    def z_of(place):
        return lax.rem(z - n.order[place] + n.Z, n.Z)

    def parts(piece, zt, place):
        first = pl.multiple_of(zt * n.qw + piece * hw, hw)
        found = [(q_ref.at[:, pl.ds(first, hw)], zb[piece].at[place, :, pl.ds(0, hw)])]
        if piece == 0:
            cols = pl.ds(pl.multiple_of(zt * HEAD, HEAD), HEAD)
            found.append((k_ref.at[:, cols], zb0.at[place, :, pl.ds(hw, HEAD)]))
            found.append((v_ref.at[:, cols], zb0.at[place, :, pl.ds(hw + HEAD, HEAD)]))
        return found

    def z_start(piece, place):
        if place == 0:
            for src, dst in parts(piece, z, 0):
                pltpu.make_async_copy(src, dst, zrecv.at[piece, 0]).start()
            return
        zt = lax.rem(z + n.order[place], n.Z)
        for src, dst in parts(piece, zt, place):
            remote(src, dst, zsend.at[piece, place], zrecv.at[piece, place], x * n.Z + zt, s)

    lane = lax.broadcasted_iota(jnp.int32, (n.flat, n.tok), 1)

    def in_run(piece, run, after=None):
        first, last = n.runs[run]
        for place in range(first, last):
            done(zb[piece].at[place], zrecv.at[piece, place])
            if after is not None:
                after(place)
            pick = (lane == idx_cols[:, place : place + 1]).astype(jnp.bfloat16)
            padded = jnp.dot(pick, zb[piece][place], preferred_element_type=jnp.float32).astype(jnp.bfloat16)
            sb[piece][:, place] = padded.reshape(n.groups, n.slots, n.widths[piece])
        run_of = pl.ds(first, last - first)
        pltpu.make_async_copy(sb[piece].at[plane, run_of], rc[piece].at[mine, run_of], precv.at[piece]).start()
        to_plane(
            lambda xt, st: remote(
                sb[piece].at[xt * n.S + st, run_of], rc[piece].at[mine, run_of],
                psend.at[piece, run], precv.at[piece], xt * n.Z + z, st,
            )
        )

    def compact(piece):
        done(rc[piece], precv.at[piece])
        sub = lax.broadcasted_iota(jnp.int32, (n.seg, n.per_s), 0)
        for k in range(n.S):
            pick = (sub == dst_rows[k : k + 1, :]).astype(jnp.bfloat16)
            block = rc[piece][k * n.X : (k + 1) * n.X].reshape(n.per_s, n.widths[piece])
            comp = jnp.dot(pick, block, preferred_element_type=jnp.float32).astype(jnp.bfloat16)
            for h in range(n.nh):
                qbuf[piece, h, k * n.seg : (k + 1) * n.seg, :] = comp[:, h * HEAD : (h + 1) * HEAD]
            if piece == 0:
                at = n.pad + k * n.seg
                kbuf[at : at + n.seg, :] = comp[:, hw : hw + HEAD]
                vbuf[at : at + n.seg, 0:HEAD] = comp[:, hw + HEAD :]

    def query_places(i, carry):
        start = pl.multiple_of(i * blk, blk)
        u = lax.broadcasted_iota(jnp.int32, (blk, 1), 0) + start
        s1 = start // n.seg
        s2 = jnp.minimum(s1 + 1, n.S - 1)
        r1 = u - s1 * n.seg
        r2 = r1 - n.seg
        one = jnp.where(r1 < tot_ref[s1], base_ref[s1] + r1, -1)
        two = jnp.where(r2 < tot_ref[s2], base_ref[s2] + r2, -1)
        pos = jnp.where(r1 < n.seg, one, two)
        ends = ends_ref[...]
        low = jnp.max(jnp.where(ends <= pos, ends, 0), axis=1, keepdims=True)
        qpos[pl.ds(start, blk), :] = jnp.broadcast_to(pos, (blk, half))
        qlow[pl.ds(start, blk), :] = jnp.broadcast_to(low, (blk, half))
        return carry

    def attend(piece, i):
        start = pl.multiple_of(i * blk, blk)
        top[...] = jnp.full(top.shape, NEG_FILL, jnp.float32)
        acc[...] = jnp.zeros(acc.shape, jnp.float32)
        chunks = (i + 4) // 4

        def at_keys(j):
            return pl.multiple_of((i + 1) * blk - wide * (j + 1) + n.pad, blk)

        def scores(j, carry):
            queries = qbuf[piece, :, pl.ds(start, blk), :].reshape(n.nh * blk, HEAD)
            sc = lax.dot_general(
                queries, kbuf[pl.ds(at_keys(j), wide), :],
                (((1,), (1,)), ((), ())), preferred_element_type=jnp.float32,
            )
            high, low = qpos[pl.ds(start, blk), :], qlow[pl.ds(start, blk), :]
            k_pos = kpos_ref[:, pl.ds(at_keys(j), wide)]
            best = top[...]
            for col in range(0, wide, half):
                here = k_pos[:, col : col + half]
                allowed = (here >= low) & (here <= high)
                part = jnp.where(
                    allowed[None], sc[:, col : col + half].reshape(n.nh, blk, half), NEG_FILL
                ).reshape(n.nh * blk, half)
                strip[j, :, col : col + half] = part
                best = jnp.maximum(best, part)
            top[...] = best
            return carry

        lax.fori_loop(0, chunks, scores, 0)
        top[...] = jnp.broadcast_to(jnp.max(top[...], axis=1, keepdims=True) * gain, top.shape)

        def weigh(j, carry):
            row = top[...]
            pieces = [
                jnp.exp2(strip[j, :, col : col + half] * gain - row).astype(jnp.bfloat16)
                for col in range(0, wide, half)
            ]
            acc[...] += jnp.dot(
                jnp.concatenate(pieces, axis=1), vbuf[pl.ds(at_keys(j), wide), :],
                preferred_element_type=jnp.float32,
            )
            return carry

        lax.fori_loop(0, chunks, weigh, 0)
        denom = acc[:, HEAD:]
        result = (acc[:, :HEAD] / jnp.where(denom > 0.0, denom, 1.0)).astype(obuf.dtype)
        for h in range(n.nh):
            obuf[pl.ds(start, blk), h * HEAD : (h + 1) * HEAD] = result[h * blk : (h + 1) * blk]

    def out_all(piece):
        wide_lane = lax.broadcasted_iota(jnp.int32, (n.per_s, n.seg), 1)
        for k in range(n.S):
            pick = (wide_lane == dst_cols[:, k : k + 1]).astype(jnp.bfloat16)
            spread = jnp.dot(
                pick, obuf[k * n.seg : (k + 1) * n.seg, :], preferred_element_type=jnp.float32
            ).astype(jnp.bfloat16)
            ub[piece, k] = spread.reshape(n.X, n.Z, n.slots, hw)
        for run in reversed(range(len(n.runs))):
            first, last = n.runs[run]
            run_of = pl.ds(first, last - first)
            pltpu.make_async_copy(
                ub.at[piece, s, x, run_of], rb.at[piece, plane, run_of], urecv.at[piece, run]
            ).start()
            to_plane(
                lambda xt, st: remote(
                    ub.at[piece, st, xt, run_of], rb.at[piece, plane, run_of],
                    usend.at[piece, run], urecv.at[piece, run], xt * n.Z + z, st,
                )
            )

    tall = lax.broadcasted_iota(jnp.int32, (n.tok, n.flat), 0)

    def hand_back(piece, run):
        first, last = n.runs[run]
        done(rb.at[piece, :, pl.ds(first, last - first)], urecv.at[piece, run])
        cols = pl.ds(pl.multiple_of(z * n.qw + piece * hw, hw), hw)
        for place in range(first, last):
            pick = (tall == idx_rows[place : place + 1, :]).astype(jnp.bfloat16)
            fb[piece, place] = jnp.dot(
                pick, rb[piece, :, place].reshape(n.flat, hw), preferred_element_type=jnp.float32
            ).astype(jnp.bfloat16)
            if place == 0:
                pltpu.make_async_copy(fb.at[piece, 0], out_ref.at[:, cols], frecv.at[piece, 0]).start()
            else:
                remote(
                    fb.at[piece, place], out_ref.at[:, cols],
                    fsend.at[piece, place], frecv.at[piece, place], x * n.Z + z_of(place), s,
                )

    places = range(n.Z)
    runs = len(n.runs)
    z_start(0, 0)
    z_start(1, 0)
    greet(n, x, z, s)
    for place in places[1:]:
        z_start(0, place)
    lax.fori_loop(0, n.nb, query_places, 0)
    kbuf[0 : n.pad, :] = jnp.zeros((n.pad, HEAD), kbuf.dtype)
    vbuf[:, 0:HEAD] = jnp.zeros((n.rows + n.pad, HEAD), vbuf.dtype)
    vbuf[:, HEAD:] = jnp.ones((n.rows + n.pad, HEAD), vbuf.dtype)

    def then_second(place):
        if place:
            z_start(1, place)

    for run in range(runs - 1):
        in_run(0, run, then_second)
    in_run(1, 0)
    in_run(0, runs - 1, then_second)
    compact(0)

    def block(t, carry):
        @pl.when(t == n.nb)
        def _():
            out_all(0)
            compact(1)

        piece = t // n.nb
        attend(piece, lax.rem(t, n.nb))
        for run in range(1, runs):

            @pl.when(t == 2 * (run - 1))
            def _(run=run):
                in_run(1, run)

        for k in range(3):

            @pl.when(t == n.nb + 3 + 3 * k)
            def _(k=k):
                if k < runs:
                    hand_back(0, runs - 1 - k)

        return carry

    lax.fori_loop(0, 2 * n.nb, block, 0)
    out_all(1)
    for run in reversed(range(max(runs - 3, 0))):
        hand_back(0, run)
    for run in reversed(range(runs)):
        hand_back(1, run)

    for piece in range(2):
        for place in places:
            done(fb.at[piece, place], frecv.at[piece, place])
            if place:
                done(fb.at[piece, place], fsend.at[piece, place])
                done(zb[piece].at[place], zsend.at[piece, place])
        for run, (first, last) in enumerate(n.runs):
            some = pl.ds(0, count - 1), pl.ds(first, last - first)
            done(sb[piece].at[some], psend.at[piece, run])
            done(rb.at[(piece,) + some], usend.at[piece, run])


def fused(n, q, k, v, idx, dst, base, tot, ends, kpos):
    smem = pl.BlockSpec(memory_space=pltpu.SMEM)
    vmem = pl.BlockSpec(memory_space=pltpu.VMEM)
    anyspace = pl.BlockSpec(memory_space=pl.ANY)
    half = min(128, n.blk)
    w0, w1 = n.widths
    chunks = (n.nb + 3) // 4
    bf, f32 = jnp.bfloat16, jnp.float32
    sem = pltpu.SemaphoreType.DMA
    runs = len(n.runs)
    senders = n.X * n.S
    return pl.pallas_call(
        functools.partial(fused_kernel, n),
        out_shape=jax.ShapeDtypeStruct((n.tok, n.Z * n.qw), bf),
        in_specs=[smem, smem, anyspace, anyspace, anyspace] + [vmem] * 6,
        out_specs=anyspace,
        scratch_shapes=[
            pltpu.VMEM((n.Z, n.tok, w0), bf),
            pltpu.VMEM((n.Z, n.tok, w1), bf),
            pltpu.VMEM((n.groups, n.Z, n.slots, w0), bf),
            pltpu.VMEM((n.groups, n.Z, n.slots, w1), bf),
            pltpu.VMEM((senders, n.Z, n.slots, w0), bf),
            pltpu.VMEM((senders, n.Z, n.slots, w1), bf),
            pltpu.VMEM((2, n.nh, n.rows, HEAD), bf),
            pltpu.VMEM((n.rows + n.pad, HEAD), bf),
            pltpu.VMEM((n.rows + n.pad, 2 * HEAD), bf),
            pltpu.VMEM((chunks, n.nh * n.blk, n.wide), f32),
            pltpu.VMEM((n.nh * n.blk, half), f32),
            pltpu.VMEM((n.nh * n.blk, 2 * HEAD), f32),
            pltpu.VMEM((n.rows, half), jnp.int32),
            pltpu.VMEM((n.rows, half), jnp.int32),
            pltpu.VMEM((n.rows, n.hw), bf),
            pltpu.VMEM((2, n.S, n.X, n.Z, n.slots, n.hw), bf),
            pltpu.VMEM((2, n.groups, n.Z, n.slots, n.hw), bf),
            pltpu.VMEM((2, n.Z, n.tok, n.hw), bf),
            sem((2, n.Z)),
            sem((2, n.Z)),
            sem((2, runs)),
            sem((2,)),
            sem((2, runs)),
            sem((2, runs)),
            sem((2, n.Z)),
            sem((2, n.Z)),
        ],
        compiler_params=pltpu.CompilerParams(
            collective_id=0, has_side_effects=True, vmem_limit_bytes=VMEM_LIMIT
        ),
        name="route_and_attend",
    )(base, tot, q, k, v, jnp.transpose(idx), idx, jnp.transpose(dst), dst, ends, kpos)


def on_device(queries, keys, values, row_offsets, doc_lengths):
    n = Sizes(
        lax.axis_size("dp"), lax.axis_size("seq"), queries.shape[0], queries.shape[1], keys.shape[1],
        row_offsets.shape[1],
    )
    dp, s = lax.axis_index("dp"), lax.axis_index("seq")
    x, z = dp // n.Z, lax.rem(dp, n.Z)
    group = x * n.S + s
    row_ends = jnp.concatenate(
        [row_offsets[:, 1:], jnp.full((row_offsets.shape[0], 1), n.tok, jnp.int32)], axis=1
    )
    counts = row_ends - row_offsets
    slot = jnp.arange(n.slots, dtype=jnp.int32)
    at_z = lax.rem(z - jnp.asarray(n.order, jnp.int32) + n.Z, n.Z)

    loader = (x * n.Z + at_z) * n.S + s
    line_starts = jnp.take(row_offsets, loader, axis=0)
    line_counts = jnp.take(counts, loader, axis=0)
    idx = jnp.where(
        slot[None, None, :] < line_counts[:, :, None], line_starts[:, :, None] + slot[None, None, :], -1
    ).reshape(n.Z, n.flat)

    column = lax.dynamic_index_in_dim(counts, group, 1, keepdims=False)
    count_grid = jnp.transpose(column.reshape(n.X * n.Z, n.S))
    tot = jnp.sum(count_grid, axis=1)
    base = jnp.cumsum(tot) - tot
    dp_base = jnp.cumsum(count_grid, axis=1) - count_grid

    def near(table):
        return jnp.take(table.reshape(n.S, n.X, n.Z), at_z, axis=2)[..., None]

    dst = jnp.where(slot < near(count_grid), near(dp_base) + slot, -1).reshape(n.S, n.per_s)
    ends = jnp.cumsum(lax.dynamic_index_in_dim(doc_lengths, group, 0, keepdims=False)).reshape(1, -1)

    r = jnp.arange(n.seg, dtype=jnp.int32)[None, :]
    kpos = jnp.where(r < tot[:, None], base[:, None] + r, BIG).reshape(1, n.rows)
    kpos = jnp.pad(kpos, ((0, 0), (n.pad, 0)), constant_values=BIG)
    return fused(n, queries, keys, values, idx, dst, base, tot, ends, kpos)


def solution(mesh):
    return jax.shard_map(
        on_device,
        mesh=mesh,
        in_specs=(P(("dp", "seq"), None), P(("dp", "seq"), None), P(("dp", "seq"), None), P(), P()),
        out_specs=P(("dp", "seq"), None),
        check_vma=False,
    )
```

time: 832 us -> 194 us (0.23)
  waiting for transfers between devices: 237 us -> 0 us
  Pallas kernels: 0 us -> 180 us
  local copies, waits for them, and re-layouts: 130 us -> 11.2 us
  loops' own time: 112 us -> 0 us
  starting transfers between devices: 106 us -> 0 us
  matrix products: 99.2 us -> 0 us
  blocking collectives: 91 us -> 0 us
  other arithmetic: 48.9 us -> 2.06 us
    all_to_all x6 -> x0, waiting for transfers between devices: 237 us -> none  [the longest x1 92.5 us: on_device(): lax.all_to_all(returned.reshape(dp_count, slot_count, width_q), 'dp', spl...]
    pallas_call x0 -> x1, Pallas kernels: none -> 180 us  [fused(): pl.pallas_call(functools.partial(fused_kernel, n), out_shape=jax.ShapeDty...]
    another operation x89 -> x0, loops' own time: 112 us -> none  [the longest x8 44.4 us: one_block(): weighted, denom = lax.fori_loop(0, q_index + 1, accumulate, start_carry)]
    all_to_all x6 -> x0, starting transfers between devices: 106 us -> none  [the longest x1 68.8 us: on_device(): lax.all_to_all(returned.reshape(dp_count, slot_count, width_q), 'dp', spl...]
    dot_general x57 -> x0, matrix products: 99.2 us -> none  [the longest x38 75.8 us: score_tile(): jnp.einsum('qhgd,khd->hgqk', q_here, k_blocks[k_index], preferred_element...]
    all_to_all x2 -> x0, blocking collectives: 91 us -> none  [the longest x1 54.6 us: on_device(): lax.all_to_all(local_out, 'seq', split_axis=0, concat_axis=1, tiled=True)]
    dynamic_slice x150 -> x2, local copies, waits for them, and re-layouts: 65 us -> 0.19 us  [the longest x1 0.18 us: on_device(): column = lax.dynamic_index_in_dim(counts, group, 1, keepdims=False)]
    and x40 -> x2, other arithmetic: 27.7 us -> 0.68 us  [the longest x1 0.67 us: near(): return jnp.take(table.reshape(n.S, n.X, n.Z), at_z, axis=2)[..., None]]
  transfers between devices with their start and end apart: 6 -> 0, of which waited for: 6 -> 0; matrix products, arithmetic and copies ran while one was open for 6% -> 0% of each run, Pallas kernels for 0% -> 0%
where the time goes in v2:
time: 194 us
  Pallas kernels  180 us (93%)
  local copies, waits for them, and re-layouts  11.2 us (6%)
  other arithmetic  2.06 us (1%)
    pallas_call x1, Pallas kernels, fused(): pl.pallas_call(functools.partial(fused_kernel, n), out_shape=jax.ShapeDty...  180 us
    unnamed x13, local copies, waits for them, and re-layouts  4.74 us

profile of v2, /device:TPU:1, one launch (start us, length us, event | category | flops | bytes accessed | tf_op | source)
XLA Modules:
  0.0 193.9 jit_solution(6137757036770145765)
XLA Ops:
  0.0 0.0 copy-start
  0.0 0.7 copy-done
  0.7 0.7 reduce-window_1_clone.1.ends_ref
  1.4 0.7 compare_and_fusion
  2.2 0.1 lt.95
  2.2 0.1 lt.89
  2.3 0.9 copy.12
  3.2 0.6 gather_fusion.1
  3.7 0.1 slice.12
  3.9 0.6 gather_fusion
  4.4 0.2 dynamic-slice_reduce_fusion
  4.6 0.1 broadcast_select_fusion.1
  4.7 0.1 reshape.113
  4.8 0.0 copy-start.3
  4.8 0.1 copy.15
  4.9 0.2 reduce-window.8
  5.1 0.0 copy-start.4
  5.1 0.2 reduce_window_sum.25
  5.3 0.1 reshape.117
  5.3 0.1 copy.18
  5.4 0.6 gather_fusion.3
  6.0 0.1 select_bitcast_fusion.2
  6.1 0.6 pad.5.kpos_ref
  6.7 0.1 reshape.116
  6.8 0.1 copy.16
  6.9 0.6 gather_fusion.2
  7.5 0.1 select_bitcast_fusion.1
  7.5 0.1 copy.17
  7.6 0.1 copy.19
  7.7 0.1 add.92
  7.8 0.1 add.93
  7.9 0.1 lt.97
  8.0 0.1 lt.98
  8.1 0.1 lt.91
  8.2 0.1 lt.92
  8.3 0.1 add.89
  8.4 0.1 add.90
  8.6 0.0 copy-start.1
  8.6 0.0 copy-start.2
  8.6 0.8 copy.20.idx_cols
  9.4 0.9 copy.21.dst_cols
  10.3 0.0 copy-done.3
  10.3 0.0 copy-done.4
  10.3 0.0 copy-done.1
  10.3 0.0 copy-done.2
  10.3 180.5 %route_and_attend.1 = bf16[256,4096]{1,0:T(8,128)(2,1)} custom-call(s32[8]{0:T(128)} %copy-done.4, s32[8]{0:T(128)} %copy-done.3, bf16[256,4096]{1,0:T(8,128)(2,1)} %q_ref.1, bf16[256,1024]{1,0:T(8,128)(2,1)} %k_ref.1, bf16[256,1024]{1,0:T(8,128)(2,1)} %v_ref.1, s32[512,8]{1,0:T(8,128)} %copy.20.idx_cols, s32[8,512]{1,0:T(8,128)} %copy-done.2, ...), custom_call_target="tpu_custom_call" | custom-call | tf_op jit(solution)/shard_map/route_and_attend/pallas_call | solution.py:340
  190.8 3.1 %copy.24 = bf16[256,4096]{1,0:T(8,128)(2,1)} copy(bf16[256,4096]{1,0:T(8,128)(2,1)} %route_and_attend.1) | data formatting | bytes 4194304
  (13 shorter events, 0.1 us)
Async XLA Ops:
  0.0 0.7 copy-start
  4.8 5.5 %copy-start.3 = (s32[8]{0:T(128)}, s32[8]{0:T(128)S(1)}, u32[]{:S(2)}) copy-start(s32[8]{0:T(128)S(1)} %reduce_sum.9.tot_ref) | copy-start | bytes 100
  5.1 5.2 %copy-start.4 = (s32[8]{0:T(128)}, s32[8]{0:T(128)S(1)}, u32[]{:S(2)}) copy-start(s32[8]{0:T(128)S(1)} %bitcast_subtract_fusion.base_ref) | copy-start | bytes 100
  8.6 1.7 copy-start.1
  8.6 1.7 copy-start.2

commit v3 on v2

v3 whole, which is shorter than its diff:
```python
import functools
import math

import jax
import jax.numpy as jnp
from jax import lax
from jax.experimental import pallas as pl
from jax.experimental.pallas import tpu as pltpu
from jax.sharding import PartitionSpec as P

MESH = pl.DeviceIdType.MESH
HEAD = 128
NEG_FILL = -1e30
BIG = 1 << 30
VMEM_LIMIT = 54 * 1024 * 1024


class Sizes:
    def __init__(self, dp_count, seq_count, tok, width_q, width_k, groups):
        self.groups = groups
        self.S = seq_count
        self.Z = width_k // HEAD
        self.X = dp_count // self.Z
        self.tok = tok
        self.slots = 2 * tok // groups
        self.seg = 3 * dp_count * tok // (2 * groups)
        self.G = width_q // width_k
        self.qw = self.G * HEAD
        self.heads = (self.G - 2, 1, 1)
        self.first_head = (0, self.G - 2, self.G - 1)
        self.widths = (self.heads[0] * HEAD + 2 * HEAD, HEAD, HEAD)
        self.flat = self.groups * self.slots
        self.per_s = self.X * self.Z * self.slots
        self.rows = self.S * self.seg
        self.blk = 2 * self.seg // 3
        self.nb = self.rows // self.blk
        self.pad = 3 * self.blk
        self.wide = 4 * self.blk
        order = [0]
        for dist in range(1, self.Z // 2 + 1):
            order.append(dist)
            if self.Z - dist != dist:
                order.append(self.Z - dist)
        self.order = order
        if self.Z == 8:
            fine = ((0, 1), (1, 3), (3, 5), (5, 7), (7, 8))
            self.in_runs = (fine, ((0, 5), (5, 8)), ((0, 5), (5, 8)))
            self.out_runs = (((5, 8), (0, 5)), ((5, 8), (0, 5)), ((5, 8), (1, 5), (0, 1)))
        else:
            runs = ((0, 1), (1, self.Z))
            self.in_runs = (runs,) * 3
            self.out_runs = (runs[::-1],) * 3


def greet(n, x, z, s):
    barrier = pltpu.get_barrier_semaphore()
    plane = x * n.S + s
    count = n.X * n.S

    def one_plane(t, carry):
        p = lax.rem(plane + t, count)
        pl.semaphore_signal(
            barrier, inc=1, device_id=((p // n.S) * n.Z + z, lax.rem(p, n.S)), device_id_type=MESH
        )
        return carry

    lax.fori_loop(1, count, one_plane, 0)

    def one_line(t, carry):
        zt = lax.rem(z + t, n.Z)
        pl.semaphore_signal(barrier, inc=1, device_id=(x * n.Z + zt, s), device_id_type=MESH)
        return carry

    lax.fori_loop(1, n.Z, one_line, 0)
    pl.semaphore_wait(barrier, count - 1 + n.Z - 1)


def fused_kernel(n, offsets_ref, lengths_ref, q_ref, k_ref, v_ref, out_ref, *scratch):
    scratch = list(scratch)

    def take(count):
        found = scratch[:count]
        del scratch[:count]
        return found

    zb, sb, rc, qbuf, ub, rb, fb = (take(3) for _ in range(7))
    kbuf, vbuf, strip, top, acc, kpos, qspan, qlow, obuf, idx_rows, idx_cols, dst_rows, dst_cols = take(13)
    zsend, zrecv, psend, precv, usend, urecv, fsend, frecv = scratch
    dp, s = lax.axis_index("dp"), lax.axis_index("seq")
    x, z = dp // n.Z, lax.rem(dp, n.Z)
    plane = x * n.S + s
    count = n.X * n.S
    mine = s * n.X + x
    blk, wide = n.blk, n.wide
    half = min(128, blk)
    gain = HEAD ** -0.5 * math.log2(math.e)
    least = -(1 << 31)
    bf, f32, i32 = jnp.bfloat16, jnp.float32, jnp.int32

    def done(ref, sem):
        pltpu.make_async_copy(ref, ref, sem).wait()

    def remote(src, dst, send, recv, dp_to, s_to):
        pltpu.make_async_remote_copy(
            src_ref=src, dst_ref=dst, send_sem=send, recv_sem=recv,
            device_id=(dp_to, s_to), device_id_type=MESH,
        ).start()

    def to_plane(body):
        def one(t, carry):
            p = lax.rem(plane + t, count)
            body(p // n.S, lax.rem(p, n.S))
            return carry

        lax.fori_loop(1, count, one, 0)

    def z_of(place):
        return lax.rem(z - n.order[place] + n.Z, n.Z)

    def z_start(piece, place):
        zt = z if place == 0 else lax.rem(z + n.order[place], n.Z)
        hw = n.heads[piece] * HEAD
        first = pl.multiple_of(zt * n.qw + n.first_head[piece] * HEAD, HEAD)
        found = [(q_ref.at[:, pl.ds(first, hw)], zb[piece].at[place, :, pl.ds(0, hw)])]
        if piece == 0:
            cols = pl.ds(pl.multiple_of(zt * HEAD, HEAD), HEAD)
            found.append((k_ref.at[:, cols], zb[0].at[place, :, pl.ds(hw, HEAD)]))
            found.append((v_ref.at[:, cols], zb[0].at[place, :, pl.ds(hw + HEAD, HEAD)]))
        for src, dst in found:
            if place == 0:
                pltpu.make_async_copy(src, dst, zrecv.at[piece, 0]).start()
            else:
                remote(src, dst, zsend.at[piece, place], zrecv.at[piece, place], x * n.Z + zt, s)

    def iota(shape, dim):
        return lax.broadcasted_iota(i32, shape, dim)

    def exact(a, b, contract):
        high = jnp.floor(a * (1.0 / 16.0)) * 16.0
        dims = (contract, ((), ()))
        return lax.dot_general(high.astype(bf), b, dims, preferred_element_type=f32) + lax.dot_general(
            (a - high).astype(bf), b, dims, preferred_element_type=f32
        )

    def tables():
        groups, flat = n.groups, n.flat
        loads = [offsets_ref[pl.ds((x * n.Z + z_of(p)) * n.S + s, 1), :] for p in range(n.Z)]
        starts = jnp.concatenate(loads, axis=0).astype(f32)
        slot_lane, slot_sub = iota((1, flat), 1), iota((flat, 1), 0)
        owner = iota((flat, groups), 0) // n.slots
        of = iota((flat, groups), 1)
        same, after = (owner == of).astype(bf), (owner + 1 == of).astype(bf)
        nt = ((1,), (1,))
        for ref, slot, swap in ((idx_rows, slot_lane, False), (idx_cols, slot_sub, True)):
            pair = []
            for table in (same, after):
                if swap:
                    pair.append(lax.dot_general(table, starts.astype(bf), (nt, ((), ())), preferred_element_type=f32))
                else:
                    pair.append(lax.dot_general(starts.astype(bf), table, (nt, ((), ())), preferred_element_type=f32))
            begin = pair[0].astype(i32) + slot % n.slots
            end = pair[1].astype(i32) + jnp.where(slot // n.slots == groups - 1, n.tok, 0)
            ref[...] = jnp.where(begin < end, begin, -1)

        devices = n.X * n.Z * n.S
        column = iota((8, groups), 1)
        sign = jnp.where(column == plane + 1, 1.0, 0.0) - jnp.where(column == plane, 1.0, 0.0)
        counts = lax.dot_general(
            sign.astype(bf), offsets_ref[...].astype(f32).astype(bf), (nt, ((), ())), preferred_element_type=f32
        ) + jnp.where(plane == groups - 1, float(n.tok), 0.0)
        fa, fb_ = iota((devices, devices), 0), iota((devices, devices), 1)
        sa, sb_ = fa % n.S, fb_ % n.S
        few = counts.astype(bf)
        before = jnp.dot(few, ((sa == sb_) & (fa < fb_)).astype(bf), preferred_element_type=f32)
        totals = jnp.dot(few, (sa == sb_).astype(bf), preferred_element_type=f32)
        bases = jnp.dot(few, (sa < sb_).astype(bf), preferred_element_type=f32)

        pick_s = (iota((n.S, devices), 1) % n.S == iota((n.S, devices), 0)).astype(f32)
        cut = pick_s * before[0:1, :]
        cut_counts = pick_s * counts[0:1, :]
        flat_s = n.per_s
        at = iota((flat_s, devices), 0) // n.slots
        place = at % n.Z
        steps = (place + 1) // 2
        shift = jnp.where(place % 2 == 1, steps, n.Z - steps)
        z_at = (z - shift + 2 * n.Z) % n.Z
        line = (((at // n.Z) * n.Z + z_at) == iota((flat_s, devices), 1) // n.S).astype(bf)
        high = jnp.floor(cut * (1.0 / 16.0)) * 16.0
        three = [a.astype(bf) for a in (high, cut - high, cut_counts)]
        for ref, swap in ((dst_rows, False), (dst_cols, True)):
            got = []
            for a in three:
                pair = (line, a) if swap else (a, line)
                got.append(lax.dot_general(*pair, (nt, ((), ())), preferred_element_type=f32))
            slot = iota((flat_s, 1), 0) if swap else iota((1, flat_s), 1)
            slot = slot % n.slots
            ref[...] = jnp.where(slot < got[2].astype(i32), (got[0] + got[1]).astype(i32) + slot, -1)

        lens = jnp.broadcast_to(lengths_ref[pl.ds(plane, 1), :].astype(f32), (8, lengths_ref.shape[1]))
        docs = lengths_ref.shape[1]
        upto = (iota((docs, docs), 0) <= iota((docs, docs), 1)).astype(bf)
        ends = exact(lens, upto, ((1,), (0,)))[0:1, :].astype(i32)
        totals, bases = totals[0:1, :].astype(i32), bases[0:1, :].astype(i32)
        kpos[:, 0 : n.pad] = jnp.full((1, n.pad), BIG + least, i32)
        for k in range(n.S):
            tot, base = totals[:, k : k + 1], bases[:, k : k + 1]
            r = iota((1, n.seg), 1)
            at = n.pad + k * n.seg
            kpos[:, at : at + n.seg] = jnp.where(r < tot, base + r, BIG) + least
            r = iota((n.seg, docs), 0)
            pos = jnp.where(r < tot, base + r, -1)
            low = jnp.max(jnp.where(ends <= pos, ends, 0), axis=1, keepdims=True)
            low = jnp.broadcast_to(low, (n.seg, half))
            r = iota((n.seg, half), 0)
            pos = jnp.where(r < tot, base + r, -1)
            qlow[k * n.seg : (k + 1) * n.seg, :] = low
            qspan[k * n.seg : (k + 1) * n.seg, :] = pos - low + least

    lane = iota((n.flat, n.tok), 1)

    def in_run(piece, run, after=None):
        first, last = n.in_runs[piece][run]
        for place in range(first, last):
            done(zb[piece].at[place], zrecv.at[piece, place])
            if after is not None and place:
                z_start(after, place)
            pick = (lane == idx_cols[:, place : place + 1]).astype(bf)
            padded = jnp.dot(pick, zb[piece][place], preferred_element_type=f32).astype(bf)
            sb[piece][:, place] = padded.reshape(n.groups, n.slots, n.widths[piece])
        run_of = pl.ds(first, last - first)
        pltpu.make_async_copy(sb[piece].at[plane, run_of], rc[piece].at[mine, run_of], precv.at[piece]).start()
        to_plane(
            lambda xt, st: remote(
                sb[piece].at[xt * n.S + st, run_of], rc[piece].at[mine, run_of],
                psend.at[piece, run], precv.at[piece], xt * n.Z + z, st,
            )
        )

    def compact(piece):
        done(rc[piece], precv.at[piece])
        sub = iota((n.seg, n.per_s), 0)
        hw = n.heads[piece] * HEAD
        for k in range(n.S):
            pick = (sub == dst_rows[k : k + 1, :]).astype(bf)
            block = rc[piece][k * n.X : (k + 1) * n.X].reshape(n.per_s, n.widths[piece])
            comp = jnp.dot(pick, block, preferred_element_type=f32).astype(bf)
            for h in range(n.heads[piece]):
                qbuf[piece][h, k * n.seg : (k + 1) * n.seg, :] = comp[:, h * HEAD : (h + 1) * HEAD]
            if piece == 0:
                at = n.pad + k * n.seg
                kbuf[at : at + n.seg, :] = comp[:, hw : hw + HEAD]
                vbuf[at : at + n.seg, 0:HEAD] = comp[:, hw + HEAD :]

    def attend(piece, i, rows):
        heads = n.heads[piece]
        start = pl.multiple_of(i * rows, rows)
        here = pl.ds(0, heads * rows)
        top[here, :] = jnp.full((heads * rows, half), NEG_FILL, f32)
        acc[here, :] = jnp.zeros((heads * rows, 2 * HEAD), f32)
        chunks = ((i + 1) * rows + wide - 1) // wide

        def at_keys(j):
            return pl.multiple_of((i + 1) * rows - wide * (j + 1) + n.pad, blk)

        def scores(j, carry):
            queries = qbuf[piece][:, pl.ds(start, rows), :].reshape(heads * rows, HEAD)
            sc = lax.dot_general(
                queries, kbuf[pl.ds(at_keys(j), wide), :], (((1,), (1,)), ((), ())), preferred_element_type=f32
            )
            span, low = qspan[pl.ds(start, rows), :], qlow[pl.ds(start, rows), :]
            k_pos = kpos[:, pl.ds(at_keys(j), wide)]
            best = top[here, :]
            for col in range(0, wide, half):
                allowed = (k_pos[:, col : col + half] - low) <= span
                part = jnp.where(
                    allowed[None], sc[:, col : col + half].reshape(heads, rows, half), NEG_FILL
                ).reshape(heads * rows, half)
                strip[j, here, col : col + half] = part
                best = jnp.maximum(best, part)
            top[here, :] = best
            return carry

        lax.fori_loop(0, chunks, scores, 0)
        top[here, :] = jnp.broadcast_to(jnp.max(top[here, :], axis=1, keepdims=True) * gain, (heads * rows, half))

        def weigh(j, carry):
            row = top[here, :]
            pieces = [
                jnp.exp2(strip[j, here, col : col + half] * gain - row).astype(bf) for col in range(0, wide, half)
            ]
            acc[here, :] += jnp.dot(
                jnp.concatenate(pieces, axis=1), vbuf[pl.ds(at_keys(j), wide), :], preferred_element_type=f32
            )
            return carry

        lax.fori_loop(0, chunks, weigh, 0)
        denom = acc[here, HEAD:]
        result = (acc[here, :HEAD] / jnp.where(denom > 0.0, denom, 1.0)).astype(bf)
        for h in range(heads):
            obuf[pl.ds(start, rows), h * HEAD : (h + 1) * HEAD] = result[h * rows : (h + 1) * rows]

    def out_all(piece):
        hw = n.heads[piece] * HEAD
        wide_lane = iota((n.per_s, n.seg), 1)
        for k in range(n.S):
            pick = (wide_lane == dst_cols[:, k : k + 1]).astype(bf)
            spread = jnp.dot(
                pick, obuf[k * n.seg : (k + 1) * n.seg, 0:hw], preferred_element_type=f32
            ).astype(bf)
            ub[piece][k] = spread.reshape(n.X, n.Z, n.slots, hw)
        for run, (first, last) in enumerate(n.out_runs[piece]):
            run_of = pl.ds(first, last - first)
            pltpu.make_async_copy(
                ub[piece].at[s, x, run_of], rb[piece].at[plane, run_of], urecv.at[piece, run]
            ).start()
            to_plane(
                lambda xt, st: remote(
                    ub[piece].at[st, xt, run_of], rb[piece].at[plane, run_of],
                    usend.at[piece, run], urecv.at[piece, run], xt * n.Z + z, st,
                )
            )

    tall = iota((n.tok, n.flat), 0)

    def hand_back(piece, run):
        first, last = n.out_runs[piece][run]
        hw = n.heads[piece] * HEAD
        done(rb[piece].at[:, pl.ds(first, last - first)], urecv.at[piece, run])
        cols = pl.ds(pl.multiple_of(z * n.qw + n.first_head[piece] * HEAD, HEAD), hw)
        for place in reversed(range(first, last)):
            pick = (tall == idx_rows[place : place + 1, :]).astype(bf)
            fb[piece][place] = jnp.dot(
                pick, rb[piece][:, place].reshape(n.flat, hw), preferred_element_type=f32
            ).astype(bf)
            if place == 0:
                pltpu.make_async_copy(fb[piece].at[0], out_ref.at[:, cols], frecv.at[piece, 0]).start()
            else:
                remote(
                    fb[piece].at[place], out_ref.at[:, cols],
                    fsend.at[piece, place], frecv.at[piece, place], x * n.Z + z_of(place), s,
                )

    for piece in range(3):
        z_start(piece, 0)
    greet(n, x, z, s)
    for place in range(1, n.Z):
        z_start(0, place)
    tables()
    kbuf[0 : n.pad, :] = jnp.zeros((n.pad, HEAD), bf)
    vbuf[:, 0:HEAD] = jnp.zeros((n.rows + n.pad, HEAD), bf)
    vbuf[:, HEAD:] = jnp.ones((n.rows + n.pad, HEAD), bf)

    for run in range(len(n.in_runs[0])):
        in_run(0, run, 1)
    compact(0)

    def with_runs(t, plan):
        for when, work in plan:

            @pl.when(t == when)
            def _(work=work):
                work()

    first_plan = (
        (2, lambda: in_run(1, 0, 2)),
        (5, lambda: in_run(1, 1, 2)),
        (7, lambda: in_run(2, 0)),
        (9, lambda: in_run(2, 1)),
    )

    def first_block(t, carry):
        attend(0, t, blk)
        with_runs(t, first_plan)
        return carry

    lax.fori_loop(0, n.nb, first_block, 0)
    out_all(0)
    compact(1)
    half_nb = n.nb // 2

    def second_block(t, carry):
        attend(1, t, 2 * blk)
        return carry

    lax.fori_loop(0, half_nb, second_block, 0)
    out_all(1)
    compact(2)
    hand_back(0, 0)

    def third_block(t, carry):
        attend(2, t, 2 * blk)
        return carry

    lax.fori_loop(0, half_nb, third_block, 0)
    out_all(2)
    for piece in range(3):
        for run in range(len(n.out_runs[piece])):
            if (piece, run) != (0, 0):
                hand_back(piece, run)

    for piece in range(3):
        for place in range(n.Z):
            done(fb[piece].at[place], frecv.at[piece, place])
            if place:
                done(fb[piece].at[place], fsend.at[piece, place])
                done(zb[piece].at[place], zsend.at[piece, place])
        for run, (first, last) in enumerate(n.in_runs[piece]):
            done(sb[piece].at[pl.ds(0, count - 1), pl.ds(first, last - first)], psend.at[piece, run])
        for run, (first, last) in enumerate(n.out_runs[piece]):
            done(rb[piece].at[pl.ds(0, count - 1), pl.ds(first, last - first)], usend.at[piece, run])


def fused(n, offsets, lengths, q, k, v):
    vmem = pl.BlockSpec(memory_space=pltpu.VMEM)
    anyspace = pl.BlockSpec(memory_space=pl.ANY)
    half = min(128, n.blk)
    chunks = (n.nb + 3) // 4
    bf, f32 = jnp.bfloat16, jnp.float32
    sem = pltpu.SemaphoreType.DMA
    senders = n.X * n.S
    outs = [h * HEAD for h in n.heads]

    def each(widths, *dims):
        return [pltpu.VMEM(dims + (w,), bf) for w in widths]

    most = max(n.heads[0] * n.blk, 2 * n.blk)
    return pl.pallas_call(
        functools.partial(fused_kernel, n),
        out_shape=jax.ShapeDtypeStruct((n.tok, n.Z * n.qw), bf),
        in_specs=[vmem, vmem, anyspace, anyspace, anyspace],
        out_specs=vmem,
        scratch_shapes=each(n.widths, n.Z, n.tok)
        + each(n.widths, n.groups, n.Z, n.slots)
        + each(n.widths, senders, n.Z, n.slots)
        + [pltpu.VMEM((h, n.rows, HEAD), bf) for h in n.heads]
        + each(outs, n.S, n.X, n.Z, n.slots)
        + each(outs, n.groups, n.Z, n.slots)
        + each(outs, n.Z, n.tok)
        + [
            pltpu.VMEM((n.rows + n.pad, HEAD), bf),
            pltpu.VMEM((n.rows + n.pad, 2 * HEAD), bf),
            pltpu.VMEM((chunks, most, n.wide), f32),
            pltpu.VMEM((most, half), f32),
            pltpu.VMEM((most, 2 * HEAD), f32),
            pltpu.VMEM((1, n.rows + n.pad), jnp.int32),
            pltpu.VMEM((n.rows, half), jnp.int32),
            pltpu.VMEM((n.rows, half), jnp.int32),
            pltpu.VMEM((n.rows, outs[0]), bf),
            pltpu.VMEM((n.Z, n.flat), jnp.int32),
            pltpu.VMEM((n.flat, n.Z), jnp.int32),
            pltpu.VMEM((n.S, n.per_s), jnp.int32),
            pltpu.VMEM((n.per_s, n.S), jnp.int32),
            sem((3, n.Z)),
            sem((3, n.Z)),
            sem((3, 5)),
            sem((3,)),
            sem((3, 5)),
            sem((3, 5)),
            sem((3, n.Z)),
            sem((3, n.Z)),
        ],
        compiler_params=pltpu.CompilerParams(
            collective_id=0, has_side_effects=True, vmem_limit_bytes=VMEM_LIMIT
        ),
        name="route_and_attend",
    )(offsets, lengths, q, k, v)


def on_device(queries, keys, values, row_offsets, doc_lengths):
    n = Sizes(
        lax.axis_size("dp"), lax.axis_size("seq"), queries.shape[0], queries.shape[1], keys.shape[1],
        row_offsets.shape[1],
    )
    return fused(n, row_offsets, doc_lengths, queries, keys, values)


def solution(mesh):
    return jax.shard_map(
        on_device,
        mesh=mesh,
        in_specs=(P(("dp", "seq"), None), P(("dp", "seq"), None), P(("dp", "seq"), None), P(), P()),
        out_specs=P(("dp", "seq"), None),
        check_vma=False,
    )
```

time: 194 us -> 189 us (0.974); the launches traced: 194 us -> 187 us
  local copies, waits for them, and re-layouts: 11.2 us -> 4.64 us
  other arithmetic: 2.06 us -> 0 us
  Pallas kernels: 180 us -> 182 us
    gather x4 -> x0, local copies, waits for them, and re-layouts: 2.27 us -> none  [the longest x2 1.16 us: near(): return jnp.take(table.reshape(n.S, n.X, n.Z), at_z, axis=2)[..., None]]
    unnamed x13 -> x2, local copies, waits for them, and re-layouts: 4.74 us -> 4.64 us
where the time goes in v3:
time: 189 us; the launch traced here: 187 us
  Pallas kernels  182 us (96%)
  local copies, waits for them, and re-layouts  4.64 us (2%)
    pallas_call x1, Pallas kernels, fused(): pl.pallas_call(functools.partial(fused_kernel, n), out_shape=jax.ShapeDty...  182 us
    unnamed x2, local copies, waits for them, and re-layouts  4.64 us

profile of v3, /device:TPU:1, one launch (start us, length us, event | category | flops | bytes accessed | tf_op | source)
XLA Modules:
  0.0 186.7 jit_solution(10349863871150857179)
XLA Ops:
  0.0 1.5 copy.6.offsets_ref
  1.5 182.1 %route_and_attend.1 = bf16[256,4096]{1,0:T(8,128)(2,1)} custom-call(s32[256,32]{1,0:T(8,128)} %copy.6.offsets_ref, s32[32,32]{1,0:T(8,128)} %lengths_ref.1, bf16[256,4096]{1,0:T(8,128)(2,1)} %q_ref.1, bf16[256,1024]{1,0:T(8,128)(2,1)} %k_ref.1, bf16[256,1024]{1,0:T(8,128)(2,1)} %v_ref.1), custom_call_target="tpu_custom_call" | custom-call | tf_op jit(solution)/shard_map/route_and_attend/pallas_call | solution.py:427
  183.6 3.1 %copy.8 = bf16[256,4096]{1,0:T(8,128)(2,1)} copy(bf16[256,4096]{1,0:T(8,128)(2,1)} %route_and_attend.1) | data formatting | bytes 4194304

commit v4 on v3

--- a/solution.py
+++ b/solution.py
@@ -12,7 +12,7 @@
 HEAD = 128
 NEG_FILL = -1e30
 BIG = 1 << 30
-VMEM_LIMIT = 54 * 1024 * 1024
+VMEM_LIMIT = 58 * 1024 * 1024
 
 
 class Sizes:
@@ -50,6 +50,13 @@
             runs = ((0, 1), (1, self.Z))
             self.in_runs = (runs,) * 3
             self.out_runs = (runs[::-1],) * 3
+        self.relay = self.X == 4 and self.S == 8
+        self.zrelay = self.Z == 8
+
+    def relayed(self, phase, piece, run):
+        if phase == 0:
+            return self.relay and (piece, run) != (0, len(self.in_runs[0]) - 1)
+        return self.relay and piece < 2
 
 
 def greet(n, x, z, s):
@@ -84,8 +91,10 @@
         return found
 
     zb, sb, rc, qbuf, ub, rb, fb = (take(3) for _ in range(7))
+    xrel = (take(3), take(3))
+    yrel = (take(3), take(3))
     kbuf, vbuf, strip, top, acc, kpos, qspan, qlow, obuf, idx_rows, idx_cols, dst_rows, dst_cols = take(13)
-    zsend, zrecv, psend, precv, usend, urecv, fsend, frecv = scratch
+    zsend, zrecv, psend, precv, usend, urecv, fsend, frecv, zrel, zs, zr, xs, xr, xf, ys, yr, yf = scratch
     dp, s = lax.axis_index("dp"), lax.axis_index("seq")
     x, z = dp // n.Z, lax.rem(dp, n.Z)
     plane = x * n.S + s
@@ -106,13 +115,89 @@
             device_id=(dp_to, s_to), device_id_type=MESH,
         ).start()
 
-    def to_plane(body):
+    y, c = s // 2, lax.rem(s, 2)
+
+    def to_plane(body, near):
         def one(t, carry):
             p = lax.rem(plane + t, count)
             body(p // n.S, lax.rem(p, n.S))
             return carry
 
-        lax.fori_loop(1, count, one, 0)
+        def one_near(t, carry):
+            dx, dy = t // 6, lax.rem(t, 6) // 2
+            dx, dy = dx + dx // 2, dy + dy // 2
+            body(lax.rem(x + dx, 4), lax.rem(y + dy, 4) * 2 + lax.rem(c + t, 2))
+            return carry
+
+        if near:
+            lax.fori_loop(1, 18, one_near, 0)
+        else:
+            lax.fori_loop(1, count, one, 0)
+
+    def side(phase, piece, run):
+        return (1, 3) if (phase + piece + run) % 2 == 0 else (3, 1)
+
+    def runs_of(phase, piece, run):
+        first, last = (n.in_runs, n.out_runs)[phase][piece][run]
+        return pl.ds(first, last - first)
+
+    def to_relays(phase, piece, run):
+        ex, ey = side(phase, piece, run)
+        part = runs_of(phase, piece, run)
+        x_far, y_far = lax.rem(x + 2, 4), lax.rem(y + 2, 4)
+        if phase == 0:
+            src = sb[piece].at[pl.ds(x_far * n.S, n.S), part]
+        else:
+            src = ub[piece].at[:, x_far, part]
+        remote(
+            src, xrel[phase][piece].at[:, part], xs.at[phase, piece, run], xr.at[phase, piece, run],
+            lax.rem(x + ex, 4) * n.Z + z, s,
+        )
+        for k, dx in enumerate((0, 1, 3)):
+            xt = lax.rem(x + dx, 4)
+            if phase == 0:
+                src = sb[piece].at[pl.ds(xt * n.S + y_far * 2, 2), part]
+            else:
+                src = ub[piece].at[pl.ds(y_far * 2, 2), xt, part]
+            remote(
+                src, yrel[phase][piece].at[k, :, part], ys.at[phase, piece, run], yr.at[phase, piece, run],
+                dp, lax.rem(y + ey, 4) * 2 + c,
+            )
+
+    def forward(phase, piece, run):
+        if not n.relayed(phase, piece, run):
+            return
+        ex, ey = side(phase, piece, run)
+        part = runs_of(phase, piece, run)
+        x_from, x_to = lax.rem(x + 4 - ex, 4), lax.rem(x + ex, 4)
+        y_from, y_to = lax.rem(y + 4 - ey, 4), lax.rem(y + ey, 4)
+
+        def landing(xo, so):
+            if phase == 0:
+                return rc[piece].at[so * n.X + xo, part], precv.at[piece]
+            return rb[piece].at[xo * n.S + so, part], urecv.at[piece, run]
+
+        done(xrel[phase][piece].at[:, part], xr.at[phase, piece, run])
+
+        def on_x(t, carry):
+            st = lax.rem(s + t, n.S)
+            dst, sem = landing(x_from, s)
+            remote(xrel[phase][piece].at[st, part], dst, xf.at[phase, piece, run], sem, x_to * n.Z + z, st)
+            return carry
+
+        lax.fori_loop(0, n.S, on_x, 0)
+        done(yrel[phase][piece].at[:, :, part], yr.at[phase, piece, run])
+
+        def on_y(t, carry):
+            k, side_c = t // 2, lax.rem(t, 2)
+            dst, sem = landing(x, y_from * 2 + c)
+            remote(
+                yrel[phase][piece].at[k, side_c, part], dst, yf.at[phase, piece, run], sem,
+                lax.rem(x + k + k // 2, 4) * n.Z + z, y_to * 2 + side_c,
+            )
+            return carry
+
+        lax.fori_loop(0, 6, on_y, 0)
 
     def z_of(place):
         return lax.rem(z - n.order[place] + n.Z, n.Z)
@@ -121,16 +206,33 @@
         zt = z if place == 0 else lax.rem(z + n.order[place], n.Z)
         hw = n.heads[piece] * HEAD
         first = pl.multiple_of(zt * n.qw + n.first_head[piece] * HEAD, HEAD)
-        found = [(q_ref.at[:, pl.ds(first, hw)], zb[piece].at[place, :, pl.ds(0, hw)])]
-        if piece == 0:
-            cols = pl.ds(pl.multiple_of(zt * HEAD, HEAD), HEAD)
-            found.append((k_ref.at[:, cols], zb[0].at[place, :, pl.ds(hw, HEAD)]))
-            found.append((v_ref.at[:, cols], zb[0].at[place, :, pl.ds(hw + HEAD, HEAD)]))
-        for src, dst in found:
+
+        def found(rows, to):
+            got = [(q_ref.at[rows, pl.ds(first, hw)], to.at[:, pl.ds(0, hw)])]
+            if piece == 0:
+                cols = pl.ds(pl.multiple_of(zt * HEAD, HEAD), HEAD)
+                got.append((k_ref.at[rows, cols], to.at[:, pl.ds(hw, HEAD)]))
+                got.append((v_ref.at[rows, cols], to.at[:, pl.ds(hw + HEAD, HEAD)]))
+            return got
+
+        if n.zrelay and (piece, place) == (0, n.Z - 1):
+            for k, via in enumerate((2, n.Z - 2)):
+                for src, dst in found(pl.ds(k * n.tok // 2, n.tok // 2), zrel.at[k]):
+                    remote(src, dst, zsend.at[0, place], zr.at[k], x * n.Z + lax.rem(z + via, n.Z), s)
+            return
+        for src, dst in found(pl.ds(0, n.tok), zb[piece].at[place]):
             if place == 0:
                 pltpu.make_async_copy(src, dst, zrecv.at[piece, 0]).start()
             else:
                 remote(src, dst, zsend.at[piece, place], zrecv.at[piece, place], x * n.Z + zt, s)
+
+    def forward_z():
+        for k, via in enumerate((2, n.Z - 2)):
+            done(zrel.at[k], zr.at[k])
+            remote(
+                zrel.at[k], zb[0].at[n.Z - 1, pl.ds(k * n.tok // 2, n.tok // 2)],
+                zs.at[k], zrecv.at[0, n.Z - 1], x * n.Z + lax.rem(z + via, n.Z), s,
+            )
 
     def iota(shape, dim):
         return lax.broadcasted_iota(i32, shape, dim)
@@ -228,12 +330,15 @@
             padded = jnp.dot(pick, zb[piece][place], preferred_element_type=f32).astype(bf)
             sb[piece][:, place] = padded.reshape(n.groups, n.slots, n.widths[piece])
         run_of = pl.ds(first, last - first)
+        if n.relayed(0, piece, run):
+            to_relays(0, piece, run)
         pltpu.make_async_copy(sb[piece].at[plane, run_of], rc[piece].at[mine, run_of], precv.at[piece]).start()
         to_plane(
             lambda xt, st: remote(
                 sb[piece].at[xt * n.S + st, run_of], rc[piece].at[mine, run_of],
                 psend.at[piece, run], precv.at[piece], xt * n.Z + z, st,
-            )
+            ),
+            n.relayed(0, piece, run),
         )
 
     def compact(piece):
@@ -310,6 +415,8 @@
             ub[piece][k] = spread.reshape(n.X, n.Z, n.slots, hw)
         for run, (first, last) in enumerate(n.out_runs[piece]):
             run_of = pl.ds(first, last - first)
+            if n.relayed(1, piece, run):
+                to_relays(1, piece, run)
             pltpu.make_async_copy(
                 ub[piece].at[s, x, run_of], rb[piece].at[plane, run_of], urecv.at[piece, run]
             ).start()
@@ -317,7 +424,8 @@
                 lambda xt, st: remote(
                     ub[piece].at[st, xt, run_of], rb[piece].at[plane, run_of],
                     usend.at[piece, run], urecv.at[piece, run], xt * n.Z + z, st,
-                )
+                ),
+                n.relayed(1, piece, run),
             )
 
     tall = iota((n.tok, n.flat), 0)
@@ -343,7 +451,7 @@
     for piece in range(3):
         z_start(piece, 0)
     greet(n, x, z, s)
-    for place in range(1, n.Z):
+    for place in (1, 2, 7, 3, 4, 5, 6) if n.zrelay else range(1, n.Z):
         z_start(0, place)
     tables()
     kbuf[0 : n.pad, :] = jnp.zeros((n.pad, HEAD), bf)
@@ -352,6 +460,10 @@
 
     for run in range(len(n.in_runs[0])):
         in_run(0, run, 1)
+        if n.zrelay and run == 1:
+            forward_z()
+        if run:
+            forward(0, 0, run - 1)
     compact(0)
 
     def with_runs(t, plan):
@@ -363,9 +475,13 @@
 
     first_plan = (
         (2, lambda: in_run(1, 0, 2)),
+        (3, lambda: forward(0, 1, 0)),
         (5, lambda: in_run(1, 1, 2)),
+        (6, lambda: forward(0, 1, 1)),
         (7, lambda: in_run(2, 0)),
+        (8, lambda: forward(0, 2, 0)),
         (9, lambda: in_run(2, 1)),
+        (10, lambda: forward(0, 2, 1)),
     )
 
     def first_block(t, carry):
@@ -380,6 +496,7 @@
 
     def second_block(t, carry):
         attend(1, t, 2 * blk)
+        with_runs(t, ((2, lambda: forward(1, 0, 0)), (4, lambda: forward(1, 0, 1))))
         return carry
 
     lax.fori_loop(0, half_nb, second_block, 0)
@@ -389,13 +506,21 @@
 
     def third_block(t, carry):
         attend(2, t, 2 * blk)
+        with_runs(
+            t,
+            (
+                (2, lambda: forward(1, 1, 0)),
+                (3, lambda: hand_back(0, 1)),
+                (4, lambda: forward(1, 1, 1)),
+            ),
+        )
         return carry
 
     lax.fori_loop(0, half_nb, third_block, 0)
     out_all(2)
     for piece in range(3):
         for run in range(len(n.out_runs[piece])):
-            if (piece, run) != (0, 0):
+            if piece:
                 hand_back(piece, run)
 
     for piece in range(3):
@@ -404,10 +529,23 @@
             if place:
                 done(fb[piece].at[place], fsend.at[piece, place])
                 done(zb[piece].at[place], zsend.at[piece, place])
-        for run, (first, last) in enumerate(n.in_runs[piece]):
-            done(sb[piece].at[pl.ds(0, count - 1), pl.ds(first, last - first)], psend.at[piece, run])
-        for run, (first, last) in enumerate(n.out_runs[piece]):
-            done(rb[piece].at[pl.ds(0, count - 1), pl.ds(first, last - first)], usend.at[piece, run])
+        for phase, runs in ((0, n.in_runs[piece]), (1, n.out_runs[piece])):
+            for run, (first, last) in enumerate(runs):
+                part = pl.ds(first, last - first)
+                relayed = n.relayed(phase, piece, run)
+                sent = pl.ds(0, 17 if relayed else count - 1)
+                if phase == 0:
+                    done(sb[piece].at[sent, part], psend.at[piece, run])
+                else:
+                    done(rb[piece].at[sent, part], usend.at[piece, run])
+                if relayed:
+                    for sem in (xs, xf):
+                        done(xrel[phase][piece].at[:, part], sem.at[phase, piece, run])
+                    for sem in (ys, yf):
+                        done(yrel[phase][piece].at[:, :, part], sem.at[phase, piece, run])
+    if n.zrelay:
+        for k in range(2):
+            done(zrel.at[k], zs.at[k])
 
 
 def fused(n, offsets, lengths, q, k, v):
@@ -436,6 +574,12 @@
         + each(outs, n.S, n.X, n.Z, n.slots)
         + each(outs, n.groups, n.Z, n.slots)
         + each(outs, n.Z, n.tok)
+        + each(n.widths, n.S, n.Z, n.slots)
+        + each(outs[:2], n.S, n.Z, n.slots)
+        + each(outs[2:], 1, 1, n.slots)
+        + each(n.widths, 3, 2, n.Z, n.slots)
+        + each(outs[:2], 3, 2, n.Z, n.slots)
+        + each(outs[2:], 1, 1, 1, n.slots)
         + [
             pltpu.VMEM((n.rows + n.pad, HEAD), bf),
             pltpu.VMEM((n.rows + n.pad, 2 * HEAD), bf),
@@ -458,7 +602,11 @@
             sem((3, 5)),
             sem((3, n.Z)),
             sem((3, n.Z)),
-        ],
+            pltpu.VMEM((2, n.tok // 2, n.widths[0]), bf),
+            sem((2,)),
+            sem((2,)),
+        ]
+        + [sem((2, 3, 5))] * 6,
         compiler_params=pltpu.CompilerParams(
             collective_id=0, has_side_effects=True, vmem_limit_bytes=VMEM_LIMIT
         ),

time: 189 us -> 205 us (1.085)
  Pallas kernels: 182 us -> 200 us
    pallas_call x1, Pallas kernels: 182 us -> 200 us  [fused(): pl.pallas_call(functools.partial(fused_kernel, n), out_shape=jax.ShapeDty...]
where the time goes in v4:
time: 205 us
  Pallas kernels  200 us (98%)
  local copies, waits for them, and re-layouts  4.64 us (2%)
    pallas_call x1, Pallas kernels, fused(): pl.pallas_call(functools.partial(fused_kernel, n), out_shape=jax.ShapeDty...  200 us
    unnamed x2, local copies, waits for them, and re-layouts  4.64 us

profile of v4, /device:TPU:1, one launch (start us, length us, event | category | flops | bytes accessed | tf_op | source)
XLA Modules:
  0.0 204.7 jit_solution(10661203831760472256)
XLA Ops:
  0.0 1.5 copy.6.offsets_ref
  1.5 200.1 %route_and_attend.1 = bf16[256,4096]{1,0:T(8,128)(2,1)} custom-call(s32[256,32]{1,0:T(8,128)} %copy.6.offsets_ref, s32[32,32]{1,0:T(8,128)} %lengths_ref.1, bf16[256,4096]{1,0:T(8,128)(2,1)} %q_ref.1, bf16[256,1024]{1,0:T(8,128)(2,1)} %k_ref.1, bf16[256,1024]{1,0:T(8,128)(2,1)} %v_ref.1), custom_call_target="tpu_custom_call" | custom-call | tf_op jit(solution)/shard_map/route_and_attend/pallas_call | solution.py:565
  201.6 3.1 %copy.8 = bf16[256,4096]{1,0:T(8,128)(2,1)} copy(bf16[256,4096]{1,0:T(8,128)(2,1)} %route_and_attend.1) | data formatting | bytes 4194304

commit v5 on v3

--- a/solution.py
+++ b/solution.py
@@ -11,7 +11,7 @@
 MESH = pl.DeviceIdType.MESH
 HEAD = 128
 NEG_FILL = -1e30
-BIG = 1 << 30
+APART = -float(1 << 40)
 VMEM_LIMIT = 54 * 1024 * 1024
 
 
@@ -26,9 +26,9 @@
         self.seg = 3 * dp_count * tok // (2 * groups)
         self.G = width_q // width_k
         self.qw = self.G * HEAD
-        self.heads = (self.G - 2, 1, 1)
-        self.first_head = (0, self.G - 2, self.G - 1)
-        self.widths = (self.heads[0] * HEAD + 2 * HEAD, HEAD, HEAD)
+        self.heads = (self.G // 2, self.G // 2)
+        self.first_head = (0, self.G // 2)
+        self.widths = (self.heads[0] * HEAD + 2 * HEAD, self.heads[1] * HEAD)
         self.flat = self.groups * self.slots
         self.per_s = self.X * self.Z * self.slots
         self.rows = self.S * self.seg
@@ -44,12 +44,12 @@
         self.order = order
         if self.Z == 8:
             fine = ((0, 1), (1, 3), (3, 5), (5, 7), (7, 8))
-            self.in_runs = (fine, ((0, 5), (5, 8)), ((0, 5), (5, 8)))
-            self.out_runs = (((5, 8), (0, 5)), ((5, 8), (0, 5)), ((5, 8), (1, 5), (0, 1)))
+            self.in_runs = (fine, ((0, 3), (3, 5), (5, 8)))
+            self.out_runs = (((5, 8), (3, 5), (0, 3)), ((7, 8), (5, 7), (3, 5), (0, 3)))
         else:
             runs = ((0, 1), (1, self.Z))
-            self.in_runs = (runs,) * 3
-            self.out_runs = (runs[::-1],) * 3
+            self.in_runs = (runs,) * 2
+            self.out_runs = (runs[::-1],) * 2
 
 
 def greet(n, x, z, s):
@@ -83,8 +83,8 @@
         del scratch[:count]
         return found
 
-    zb, sb, rc, qbuf, ub, rb, fb = (take(3) for _ in range(7))
-    kbuf, vbuf, strip, top, acc, kpos, qspan, qlow, obuf, idx_rows, idx_cols, dst_rows, dst_cols = take(13)
+    zb, sb, rc, qbuf, ub, rb, fb = (take(2) for _ in range(7))
+    kbuf, vbuf, qdoc, strip, top, acc, obuf, idx_rows, idx_cols, dst_rows, dst_cols = take(11)
     zsend, zrecv, psend, precv, usend, urecv, fsend, frecv = scratch
     dp, s = lax.axis_index("dp"), lax.axis_index("seq")
     x, z = dp // n.Z, lax.rem(dp, n.Z)
@@ -94,7 +94,6 @@
     blk, wide = n.blk, n.wide
     half = min(128, blk)
     gain = HEAD ** -0.5 * math.log2(math.e)
-    least = -(1 << 31)
     bf, f32, i32 = jnp.bfloat16, jnp.float32, jnp.int32
 
     def done(ref, sem):
@@ -107,12 +106,16 @@
         ).start()
 
     def to_plane(body):
-        def one(t, carry):
-            p = lax.rem(plane + t, count)
-            body(p // n.S, lax.rem(p, n.S))
+        for ds in range(1, n.S):
+            body(x, lax.rem(s + ds, n.S))
+
+        def one(dx, carry):
+            xt = lax.rem(x + dx, n.X)
+            for ds in range(n.S):
+                body(xt, lax.rem(s + ds, n.S))
             return carry
 
-        lax.fori_loop(1, count, one, 0)
+        lax.fori_loop(1, n.X, one, 0)
 
     def z_of(place):
         return lax.rem(z - n.order[place] + n.Z, n.Z)
@@ -201,20 +204,18 @@
         upto = (iota((docs, docs), 0) <= iota((docs, docs), 1)).astype(bf)
         ends = exact(lens, upto, ((1,), (0,)))[0:1, :].astype(i32)
         totals, bases = totals[0:1, :].astype(i32), bases[0:1, :].astype(i32)
-        kpos[:, 0 : n.pad] = jnp.full((1, n.pad), BIG + least, i32)
+        kind = iota((n.seg, HEAD), 1)
+        kbuf[0 : n.pad, HEAD:] = (kind[0:1, :] == HEAD - 1).astype(bf) + jnp.zeros((n.pad, HEAD), bf)
         for k in range(n.S):
             tot, base = totals[:, k : k + 1], bases[:, k : k + 1]
-            r = iota((1, n.seg), 1)
-            at = n.pad + k * n.seg
-            kpos[:, at : at + n.seg] = jnp.where(r < tot, base + r, BIG) + least
             r = iota((n.seg, docs), 0)
-            pos = jnp.where(r < tot, base + r, -1)
-            low = jnp.max(jnp.where(ends <= pos, ends, 0), axis=1, keepdims=True)
-            low = jnp.broadcast_to(low, (n.seg, half))
-            r = iota((n.seg, half), 0)
-            pos = jnp.where(r < tot, base + r, -1)
-            qlow[k * n.seg : (k + 1) * n.seg, :] = low
-            qspan[k * n.seg : (k + 1) * n.seg, :] = pos - low + least
+            doc = jnp.sum(jnp.where(ends <= base + r, 1.0, 0.0), axis=1, keepdims=True)
+            doc = jnp.broadcast_to(doc, (n.seg, HEAD)).astype(i32)
+            real = iota((n.seg, HEAD), 0) < tot
+            rows = slice(k * n.seg, (k + 1) * n.seg)
+            qdoc[rows, :] = jnp.where(kind == jnp.where(real, doc, HEAD - 2), 0.0, APART).astype(bf)
+            rows = slice(n.pad + k * n.seg, n.pad + (k + 1) * n.seg)
+            kbuf[rows, HEAD:] = jnp.where(kind == jnp.where(real, doc, HEAD - 1), 1.0, 0.0).astype(bf)
 
     lane = iota((n.flat, n.tok), 1)
 
@@ -248,7 +249,7 @@
                 qbuf[piece][h, k * n.seg : (k + 1) * n.seg, :] = comp[:, h * HEAD : (h + 1) * HEAD]
             if piece == 0:
                 at = n.pad + k * n.seg
-                kbuf[at : at + n.seg, :] = comp[:, hw : hw + HEAD]
+                kbuf[at : at + n.seg, 0:HEAD] = comp[:, hw : hw + HEAD]
                 vbuf[at : at + n.seg, 0:HEAD] = comp[:, hw + HEAD :]
 
     def attend(piece, i, rows):
@@ -262,25 +263,37 @@
         def at_keys(j):
             return pl.multiple_of((i + 1) * rows - wide * (j + 1) + n.pad, blk)
 
-        def scores(j, carry):
-            queries = qbuf[piece][:, pl.ds(start, rows), :].reshape(heads * rows, HEAD)
+        def scores(j, diagonal):
+            doc = qdoc[pl.ds(start, rows), :]
+            queries = jnp.concatenate(
+                [
+                    qbuf[piece][:, pl.ds(start, rows), :].reshape(heads * rows, HEAD),
+                    jnp.concatenate([doc] * heads, axis=0),
+                ],
+                axis=1,
+            )
             sc = lax.dot_general(
                 queries, kbuf[pl.ds(at_keys(j), wide), :], (((1,), (1,)), ((), ())), preferred_element_type=f32
             )
-            span, low = qspan[pl.ds(start, rows), :], qlow[pl.ds(start, rows), :]
-            k_pos = kpos[:, pl.ds(at_keys(j), wide)]
             best = top[here, :]
             for col in range(0, wide, half):
-                allowed = (k_pos[:, col : col + half] - low) <= span
-                part = jnp.where(
-                    allowed[None], sc[:, col : col + half].reshape(heads, rows, half), NEG_FILL
-                ).reshape(heads * rows, half)
+                part = sc[:, col : col + half]
+                if diagonal and col >= wide - rows:
+                    later = iota((rows, half), 1) + (col - wide + rows) > iota((rows, half), 0)
+                    part = jnp.where(later[None], NEG_FILL, part.reshape(heads, rows, half)).reshape(
+                        heads * rows, half
+                    )
                 strip[j, here, col : col + half] = part
                 best = jnp.maximum(best, part)
             top[here, :] = best
+
+        scores(0, True)
+
+        def more(j, carry):
+            scores(j, False)
             return carry
 
-        lax.fori_loop(0, chunks, scores, 0)
+        lax.fori_loop(1, chunks, more, 0)
         top[here, :] = jnp.broadcast_to(jnp.max(top[here, :], axis=1, keepdims=True) * gain, (heads * rows, half))
 
         def weigh(j, carry):
@@ -340,13 +353,13 @@
                     fsend.at[piece, place], frecv.at[piece, place], x * n.Z + z_of(place), s,
                 )
 
-    for piece in range(3):
+    for piece in range(2):
         z_start(piece, 0)
     greet(n, x, z, s)
     for place in range(1, n.Z):
         z_start(0, place)
     tables()
-    kbuf[0 : n.pad, :] = jnp.zeros((n.pad, HEAD), bf)
+    kbuf[0 : n.pad, 0:HEAD] = jnp.zeros((n.pad, HEAD), bf)
     vbuf[:, 0:HEAD] = jnp.zeros((n.rows + n.pad, HEAD), bf)
     vbuf[:, HEAD:] = jnp.ones((n.rows + n.pad, HEAD), bf)
 
@@ -361,12 +374,7 @@
             def _(work=work):
                 work()
 
-    first_plan = (
-        (2, lambda: in_run(1, 0, 2)),
-        (5, lambda: in_run(1, 1, 2)),
-        (7, lambda: in_run(2, 0)),
-        (9, lambda: in_run(2, 1)),
-    )
+    first_plan = [(2 + 3 * k, functools.partial(in_run, 1, k)) for k in range(len(n.in_runs[1]))]
 
     def first_block(t, carry):
         attend(0, t, blk)
@@ -376,29 +384,21 @@
     lax.fori_loop(0, n.nb, first_block, 0)
     out_all(0)
     compact(1)
-    half_nb = n.nb // 2
+    second_plan = [(5 + 3 * k, functools.partial(hand_back, 0, k)) for k in range(min(2, len(n.out_runs[0])))]
 
     def second_block(t, carry):
-        attend(1, t, 2 * blk)
+        attend(1, t, blk)
+        with_runs(t, second_plan)
         return carry
 
-    lax.fori_loop(0, half_nb, second_block, 0)
+    lax.fori_loop(0, n.nb, second_block, 0)
     out_all(1)
-    compact(2)
-    hand_back(0, 0)
-
-    def third_block(t, carry):
-        attend(2, t, 2 * blk)
-        return carry
-
-    lax.fori_loop(0, half_nb, third_block, 0)
-    out_all(2)
-    for piece in range(3):
-        for run in range(len(n.out_runs[piece])):
-            if (piece, run) != (0, 0):
-                hand_back(piece, run)
-
-    for piece in range(3):
+    for run in range(2, len(n.out_runs[0])):
+        hand_back(0, run)
+    for run in range(len(n.out_runs[1])):
+        hand_back(1, run)
+
+    for piece in range(2):
         for place in range(n.Z):
             done(fb[piece].at[place], frecv.at[piece, place])
             if place:
@@ -423,7 +423,7 @@
     def each(widths, *dims):
         return [pltpu.VMEM(dims + (w,), bf) for w in widths]
 
-    most = max(n.heads[0] * n.blk, 2 * n.blk)
+    most = n.heads[0] * n.blk
     return pl.pallas_call(
         functools.partial(fused_kernel, n),
         out_shape=jax.ShapeDtypeStruct((n.tok, n.Z * n.qw), bf),
@@ -437,27 +437,25 @@
         + each(outs, n.groups, n.Z, n.slots)
         + each(outs, n.Z, n.tok)
         + [
-            pltpu.VMEM((n.rows + n.pad, HEAD), bf),
             pltpu.VMEM((n.rows + n.pad, 2 * HEAD), bf),
+            pltpu.VMEM((n.rows + n.pad, 2 * HEAD), bf),
+            pltpu.VMEM((n.rows, HEAD), bf),
             pltpu.VMEM((chunks, most, n.wide), f32),
             pltpu.VMEM((most, half), f32),
             pltpu.VMEM((most, 2 * HEAD), f32),
-            pltpu.VMEM((1, n.rows + n.pad), jnp.int32),
-            pltpu.VMEM((n.rows, half), jnp.int32),
-            pltpu.VMEM((n.rows, half), jnp.int32),
             pltpu.VMEM((n.rows, outs[0]), bf),
             pltpu.VMEM((n.Z, n.flat), jnp.int32),
             pltpu.VMEM((n.flat, n.Z), jnp.int32),
             pltpu.VMEM((n.S, n.per_s), jnp.int32),
             pltpu.VMEM((n.per_s, n.S), jnp.int32),
-            sem((3, n.Z)),
-            sem((3, n.Z)),
-            sem((3, 5)),
-            sem((3,)),
-            sem((3, 5)),
-            sem((3, 5)),
-            sem((3, n.Z)),
-            sem((3, n.Z)),
+            sem((2, n.Z)),
+            sem((2, n.Z)),
+            sem((2, 5)),
+            sem((2,)),
+            sem((2, 5)),
+            sem((2, 5)),
+            sem((2, n.Z)),
+            sem((2, n.Z)),
         ],
         compiler_params=pltpu.CompilerParams(
             collective_id=0, has_side_effects=True, vmem_limit_bytes=VMEM_LIMIT

time: 189 us -> 179 us (0.947); the launches traced: 187 us -> 179 us
  Pallas kernels: 182 us -> 174 us
    pallas_call x1, Pallas kernels: 182 us -> 174 us  [fused(): pl.pallas_call(functools.partial(fused_kernel, n), out_shape=jax.ShapeDty...]
where the time goes in v5:
time: 179 us
  Pallas kernels  174 us (97%)
  local copies, waits for them, and re-layouts  4.64 us (3%)
    pallas_call x1, Pallas kernels, fused(): pl.pallas_call(functools.partial(fused_kernel, n), out_shape=jax.ShapeDty...  174 us
    unnamed x2, local copies, waits for them, and re-layouts  4.64 us

profile of v5, /device:TPU:1, one launch (start us, length us, event | category | flops | bytes accessed | tf_op | source)
XLA Modules:
  0.0 179.1 jit_solution(587875646548219388)
XLA Ops:
  0.0 1.5 copy.6.offsets_ref
  1.5 174.5 %route_and_attend.1 = bf16[256,4096]{1,0:T(8,128)(2,1)} custom-call(s32[256,32]{1,0:T(8,128)} %copy.6.offsets_ref, s32[32,32]{1,0:T(8,128)} %lengths_ref.1, bf16[256,4096]{1,0:T(8,128)(2,1)} %q_ref.1, bf16[256,1024]{1,0:T(8,128)(2,1)} %k_ref.1, bf16[256,1024]{1,0:T(8,128)(2,1)} %v_ref.1), custom_call_target="tpu_custom_call" | custom-call | tf_op jit(solution)/shard_map/route_and_attend/pallas_call | solution.py:427
  176.0 3.1 %copy.8 = bf16[256,4096]{1,0:T(8,128)(2,1)} copy(bf16[256,4096]{1,0:T(8,128)(2,1)} %route_and_attend.1) | data formatting | bytes 4194304

commit v6 on v5

--- a/solution.py
+++ b/solution.py
@@ -12,7 +12,7 @@
 HEAD = 128
 NEG_FILL = -1e30
 APART = -float(1 << 40)
-VMEM_LIMIT = 54 * 1024 * 1024
+VMEM_LIMIT = 50 * 1024 * 1024
 
 
 class Sizes:
@@ -147,8 +147,13 @@
 
     def tables():
         groups, flat = n.groups, n.flat
-        loads = [offsets_ref[pl.ds((x * n.Z + z_of(p)) * n.S + s, 1), :] for p in range(n.Z)]
-        starts = jnp.concatenate(loads, axis=0).astype(f32)
+        devices = n.X * n.Z * n.S
+        offsets = offsets_ref[...].astype(f32).astype(bf)
+        which = iota((n.Z, devices), 0)
+        steps = (which + 1) // 2
+        which = (z - jnp.where(which % 2 == 1, steps, n.Z - steps) + 2 * n.Z) % n.Z
+        line_of = (iota((n.Z, devices), 1) == (x * n.Z + which) * n.S + s).astype(bf)
+        starts = lax.dot_general(line_of, offsets, (((1,), (1,)), ((), ())), preferred_element_type=f32)
         slot_lane, slot_sub = iota((1, flat), 1), iota((flat, 1), 0)
         owner = iota((flat, groups), 0) // n.slots
         of = iota((flat, groups), 1)
@@ -165,11 +170,10 @@
             end = pair[1].astype(i32) + jnp.where(slot // n.slots == groups - 1, n.tok, 0)
             ref[...] = jnp.where(begin < end, begin, -1)
 
-        devices = n.X * n.Z * n.S
         column = iota((8, groups), 1)
         sign = jnp.where(column == plane + 1, 1.0, 0.0) - jnp.where(column == plane, 1.0, 0.0)
         counts = lax.dot_general(
-            sign.astype(bf), offsets_ref[...].astype(f32).astype(bf), (nt, ((), ())), preferred_element_type=f32
+            sign.astype(bf), offsets, (((1,), (0,)), ((), ())), preferred_element_type=f32
         ) + jnp.where(plane == groups - 1, float(n.tok), 0.0)
         fa, fb_ = iota((devices, devices), 0), iota((devices, devices), 1)
         sa, sb_ = fa % n.S, fb_ % n.S
@@ -428,7 +432,7 @@
         functools.partial(fused_kernel, n),
         out_shape=jax.ShapeDtypeStruct((n.tok, n.Z * n.qw), bf),
         in_specs=[vmem, vmem, anyspace, anyspace, anyspace],
-        out_specs=vmem,
+        out_specs=anyspace,
         scratch_shapes=each(n.widths, n.Z, n.tok)
         + each(n.widths, n.groups, n.Z, n.slots)
         + each(n.widths, senders, n.Z, n.slots)
@@ -469,7 +473,7 @@
         lax.axis_size("dp"), lax.axis_size("seq"), queries.shape[0], queries.shape[1], keys.shape[1],
         row_offsets.shape[1],
     )
-    return fused(n, row_offsets, doc_lengths, queries, keys, values)
+    return fused(n, jnp.transpose(row_offsets), doc_lengths, queries, keys, values)
 
 
 def solution(mesh):

time: 179 us -> 178 us (level)
  Pallas kernels: 174 us -> 172 us
    pallas_call x1, Pallas kernels: 174 us -> 172 us  [fused(): pl.pallas_call(functools.partial(fused_kernel, n), out_shape=jax.ShapeDty...]
    unnamed x2 -> x9, local copies, waits for them, and re-layouts: 4.64 us -> 4.88 us
where the time goes in v6:
time: 178 us; the launch traced here: 177 us
  Pallas kernels  172 us (97%)
  local copies, waits for them, and re-layouts  4.88 us (3%)
    pallas_call x1, Pallas kernels, fused(): pl.pallas_call(functools.partial(fused_kernel, n), out_shape=jax.ShapeDty...  172 us
    unnamed x9, local copies, waits for them, and re-layouts  4.88 us

profile of v6, /device:TPU:1, one launch (start us, length us, event | category | flops | bytes accessed | tf_op | source)
XLA Modules:
  0.0 177.3 jit_solution(8182954168229495070)
XLA Ops:
  0.0 0.0 copy-start
  0.0 1.0 copy-done
  1.0 0.0 copy-start.1
  1.0 1.0 copy-done.1
  2.1 0.0 copy-start.2
  2.1 0.8 copy-done.2
  2.8 0.0 copy-start.3
  2.8 0.7 copy-done.3
  3.6 172.4 %route_and_attend.1 = bf16[256,4096]{1,0:T(8,128)(2,1)S(1)} custom-call(s32[32,256]{1,0:T(8,128)S(1)} %bitcast.1, s32[32,32]{1,0:T(8,128)S(1)} %copy-done.3, bf16[256,4096]{1,0:T(8,128)(2,1)} %q_ref.1, bf16[256,1024]{1,0:T(8,128)(2,1)S(1)} %copy-done, bf16[256,1024]{1,0:T(8,128)(2,1)S(1)} %copy-done.1), custom_call_target="tpu_custom_call" | custom-call | tf_op jit(solution)/shard_map/route_and_attend/pallas_call | solution.py:431
  176.0 1.3 copy.7
Async XLA Ops:
  0.0 1.0 copy-start
  1.0 1.0 copy-start.1
  2.1 0.8 copy-start.2
  2.8 0.7 copy-start.3
